TPU v7x, 32 devices: a whole 2x2x4 slice. The times are simulated.
32 devices in a mesh: ctx: 8 (over z, x), head: 4 (over y, core).
Axes of the slice: x: 2, y: 2, z: 4, core: 2. Of those that a mesh axis runs over, the one named last changes fastest.
Arguments:
- tokens: bfloat16 [2, 4096, 2048], P(None, 'ctx', 'head'), may hold values from -6 to 6
- region_lengths: int32 [2, 64], replicated, may hold values from 1 to 256, 4096 in all within a row
- header_lengths: int32 [2, 64], replicated, may hold values from 1 to 32
- w_query: bfloat16 [2048, 2048], P(None, 'head'), may hold values from -0.125 to 0.125
- w_key: bfloat16 [2048, 2048], P(None, 'head'), may hold values from -0.125 to 0.125
- w_value: bfloat16 [2048, 4096], P(None, 'head'), may hold values from -0.125 to 0.125
- w_gate: bfloat16 [2048, 4096], P(None, 'head'), may hold values from -0.125 to 0.125
- w_decay: bfloat16 [2048, 32], P(None, 'head'), may hold values from -0.125 to 0.125
- w_beta: bfloat16 [2048, 32], P(None, 'head'), may hold values from -0.125 to 0.125
- conv_query: float32 [4, 2048], P(None, 'head'), may hold values from -3 to 3
- conv_key: float32 [4, 2048], P(None, 'head'), may hold values from -3 to 3
- conv_value: float32 [4, 4096], P(None, 'head'), may hold values from -3 to 3
- decay_rate: float32 [32], P('head'), may hold values from 6.1035156e-05 to 0.1
- decay_bias: float32 [32], P('head'), may hold values from -2 to 1
- beta_bias: float32 [32], P('head'), may hold values from -6.5 to 1
- norm_gain: float32 [128], replicated, may hold values from 0.1 to 1.9
- w_out: bfloat16 [4096, 2048], P('head'), may hold values from -0.09375 to 0.09375
Outputs:
- mixed: bfloat16 [2, 4096, 2048], P(None, ('ctx', 'head'))
Inputs may be any that keep to these rules, and one draw needn't show every extreme that they name: `region_lengths`: each row sums to 4096; the longest region has exactly 256 positions.
All inputs are finite; a program needn't handle non-finite values.
Results may differ from a plain program's by a relative error of at most 0.013.
Values may be sent and summed in bfloat16 or wider, within the bound.
A program may use at most 192 MiB of HBM per device.

v0:
```python
import jax
import jax.numpy as jnp
from jax import lax
from jax.sharding import PartitionSpec as P

GROUP = 64


HIGH = lax.Precision.HIGHEST


def shifted(shard, axis, by):
    length = lax.axis_size(axis)
    pairs = [(i, i + by) for i in range(length) if 0 <= i + by < length]
    return lax.ppermute(shard, axis, pairs)


def product(form, left, right):
    return jnp.einsum(form, left, right, precision=HIGH)


def region_masks(position, region_lengths, header_lengths):
    ends = jnp.cumsum(region_lengths, axis=1)
    starts = ends - region_lengths
    span = jnp.minimum(header_lengths, region_lengths)
    inside = (position[None, None, :] >= starts[:, :, None]) & (
        position[None, None, :] < ends[:, :, None]
    )
    header = inside & (position[None, None, :] < (starts + span)[:, :, None])
    return (inside, header, span)


def causal_conv(sequence, kernel, rim):
    extended = jnp.concatenate([rim, sequence], axis=1).astype(jnp.float32)
    width = kernel.shape[0]
    length = sequence.shape[1]
    total = kernel[0] * extended[:, 0:length]
    for offset in range(1, width):
        total = total + kernel[offset] * extended[:, offset : offset + length]
    return jax.nn.silu(total)


def unit_rows(rows, factor):
    return rows * lax.rsqrt(jnp.sum(rows * rows, axis=-1, keepdims=True) + 1e-06) * factor


def group_terms(queries, key_rows, value_rows, log_decay, strength):
    size = queries.shape[-2]
    dim_value = value_rows.shape[-1]
    dim_key = key_rows.shape[-1]
    cumul = jnp.cumsum(log_decay, axis=-1)
    places = jnp.arange(size)
    incl = places[:, None] >= places[None, :]
    strict = places[:, None] > places[None, :]
    spread = cumul[..., :, None] - cumul[..., None, :]
    ratio = jnp.where(incl, jnp.exp(jnp.where(incl, spread, 0.0)), 0.0)
    key_key = product("...td,...jd->...tj", key_rows, key_rows)
    lower = jnp.where(strict, ratio * key_key * strength[..., :, None], 0.0)
    system = lower + jnp.eye(size, dtype=jnp.float32)
    scaled = jnp.exp(cumul)[..., None]
    right_side = strength[..., None] * jnp.concatenate([value_rows, scaled * key_rows], axis=-1)
    solved = jax.scipy.linalg.solve_triangular(system, right_side, lower=True, unit_diagonal=True)
    local_u = solved[..., :dim_value]
    weights_w = solved[..., dim_value:]
    tail_keys = jnp.exp(cumul[..., -1:] - cumul)[..., None] * key_rows
    last_decay = jnp.exp(cumul[..., -1])
    transition = last_decay[..., None, None] * jnp.eye(dim_key, dtype=jnp.float32) - product(
        "...td,...te->...de", tail_keys, weights_w
    )
    offset_map = product("...td,...te->...de", tail_keys, local_u)
    attend = ratio * product("...td,...jd->...tj", queries, key_rows)
    query_eff = scaled * queries - product("...tj,...jd->...td", attend, weights_w)
    base_out = product("...tj,...jd->...td", attend, local_u)
    return (transition, offset_map, query_eff, base_out)


def gated_norm(outputs, gate_raw, norm_gain):
    mean_sq = jnp.mean(outputs * outputs, axis=-1, keepdims=True)
    gate_val = jax.nn.silu(gate_raw.astype(jnp.float32))
    return outputs * lax.rsqrt(mean_sq + 1e-06) * norm_gain * gate_val


def per_device(
    tokens,
    region_lengths,
    header_lengths,
    w_query,
    w_key,
    w_value,
    w_gate,
    w_decay,
    w_beta,
    conv_query,
    conv_key,
    conv_value,
    decay_rate,
    decay_bias,
    beta_bias,
    norm_gain,
    w_out,
):
    seq_count, tok_count, width_part = tokens.shape
    head_dim = norm_gain.shape[0]
    conv_width = conv_query.shape[0]
    value_heads = w_decay.shape[1]
    qk_heads = w_query.shape[1] // head_dim
    position = lax.axis_index("ctx") * tok_count + jnp.arange(tok_count, dtype=jnp.int32)
    inside, header, span = region_masks(position, region_lengths, header_lengths)
    tokens_wide = tokens.astype(jnp.float32)
    partial_sums = product("srt,std->srd", header.astype(jnp.float32), tokens_wide)
    totals = lax.psum(partial_sums, "ctx")
    means = totals / span[..., None].astype(jnp.float32)
    augmented = (tokens_wide + product("srt,srd->std", inside.astype(jnp.float32), means)).astype(
        jnp.bfloat16
    )
    weights = (w_query, w_key, w_value, w_gate, w_decay, w_beta)
    whole = lax.all_gather(augmented, "head", axis=2, tiled=True)
    projected = tuple(
        (
            jnp.einsum("std,de->ste", whole, weight, preferred_element_type=jnp.float32)
            for weight in weights
        )
    )
    query_raw = projected[0].astype(jnp.bfloat16)
    key_raw = projected[1].astype(jnp.bfloat16)
    value_raw = projected[2].astype(jnp.bfloat16)
    gate_raw = projected[3].astype(jnp.bfloat16)
    decay_logit = projected[4]
    beta_logit = projected[5]
    mixed_raw = jnp.concatenate([query_raw, key_raw, value_raw], axis=-1)
    kernel = jnp.concatenate([conv_query, conv_key, conv_value], axis=-1)
    rim = shifted(mixed_raw[:, tok_count - (conv_width - 1) :, :], "ctx", 1)
    convolved = causal_conv(mixed_raw, kernel, rim)
    qk_width = w_query.shape[1]
    queries = unit_rows(
        convolved[..., :qk_width].reshape(seq_count, tok_count, qk_heads, head_dim),
        head_dim ** (-0.5),
    )
    key_rows = unit_rows(
        convolved[..., qk_width : 2 * qk_width].reshape(seq_count, tok_count, qk_heads, head_dim),
        1.0,
    )
    value_rows = convolved[..., 2 * qk_width :].reshape(seq_count, tok_count, value_heads, head_dim)
    queries = jnp.repeat(queries, 2, axis=2)
    key_rows = jnp.repeat(key_rows, 2, axis=2)
    log_decay = -decay_rate * jax.nn.softplus(decay_logit + decay_bias)
    strength = jax.nn.sigmoid(beta_logit + beta_bias)
    blocks = tok_count // GROUP

    def cut_four(array):
        return array.reshape(seq_count, blocks, GROUP, value_heads, head_dim).transpose(
            0, 3, 1, 2, 4
        )

    def cut_three(array):
        return array.reshape(seq_count, blocks, GROUP, value_heads).transpose(0, 3, 1, 2)

    transition, offset_map, query_eff, base_out = group_terms(
        cut_four(queries),
        cut_four(key_rows),
        cut_four(value_rows),
        cut_three(log_decay),
        cut_three(strength),
    )
    identity = jnp.broadcast_to(
        jnp.eye(head_dim, dtype=jnp.float32), (seq_count, value_heads, head_dim, head_dim)
    )
    zero_state = jnp.zeros((seq_count, value_heads, head_dim, head_dim), jnp.float32)

    def advance(carried, items):
        running_a, running_b = carried
        trans_now, offset_now = items
        updated = (
            product("shde,shef->shdf", trans_now, running_a),
            product("shde,shef->shdf", trans_now, running_b) + offset_now,
        )
        return (updated, (running_a, running_b))

    (device_a, device_b), (before_a, before_b) = lax.scan(
        advance,
        (identity, zero_state),
        (jnp.moveaxis(transition, 2, 0), jnp.moveaxis(offset_map, 2, 0)),
    )
    before_a = jnp.moveaxis(before_a, 0, 2)
    before_b = jnp.moveaxis(before_b, 0, 2)
    query_total = product("shntd,shnde->shnte", query_eff, before_a)
    base_total = product("shntd,shnde->shnte", query_eff, before_b) + base_out

    def relay(counter, incoming):
        return shifted(product("shde,shef->shdf", device_a, incoming) + device_b, "ctx", 1)

    state_in = lax.fori_loop(0, lax.axis_size("ctx") - 1, relay, zero_state)
    outputs = product("shntd,shde->shnte", query_total, state_in) + base_total
    outputs = outputs.transpose(0, 2, 3, 1, 4).reshape(seq_count, tok_count, value_heads, head_dim)
    normed = gated_norm(
        outputs, gate_raw.reshape(seq_count, tok_count, value_heads, head_dim), norm_gain
    )
    hidden = jnp.swapaxes(
        normed.astype(jnp.bfloat16).reshape(seq_count, tok_count, value_heads * head_dim), 0, 1
    )
    mixed = lax.psum_scatter(
        jnp.einsum("tse,ed->tsd", hidden, w_out, preferred_element_type=jnp.float32),
        "head",
        scatter_dimension=0,
        tiled=True,
    )
    return jnp.swapaxes(mixed, 0, 1).astype(jnp.bfloat16)


def solution(mesh):
    return jax.shard_map(
        per_device,
        mesh=mesh,
        in_specs=(
            P(None, "ctx", "head"),
            P(),
            P(),
            P(None, "head"),
            P(None, "head"),
            P(None, "head"),
            P(None, "head"),
            P(None, "head"),
            P(None, "head"),
            P(None, "head"),
            P(None, "head"),
            P(None, "head"),
            P("head"),
            P("head"),
            P("head"),
            P(),
            P("head", None),
        ),
        out_specs=P(None, ("ctx", "head"), None),
        check_vma=False,
    )
```

profile of v0, /device:TPU:0, one launch (start us, length us, event | category | flops | bytes accessed | tf_op | source)
XLA Modules:
  0.0 1302.1 jit_solution(13613279907648917407)
XLA Ops:
  10.7 73.4 %all-reduce.2.cloned.1.call-done = f32[2,64,512]{2,1,0:T(8,128)} async-done(((f32[2,64,512]{2,1,0:T(8,128)}), f32[2,64,512]{2,1,0:T(8,128)}) %all-reduce.2.cloned.1.call-update) | async-done | bytes 262160 | tf_op jit(solution)/shard_map/psum | solution.py:111
  84.1 3.5 add_convert_fusion
  90.9 30.6 %all-gather.2.cloned.1.call-done = bf16[2,512,2048]{2,1,0:T(8,128)(2,1)} async-done(((bf16[2,512,512]{2,1,0:T(8,128)(2,1)}), bf16[2,512,2048]{2,1,0:T(8,128)(2,1)}) %all-gather.2.cloned.1.call-update) | async-done | bytes 4194320 | tf_op jit(solution)/shard_map/all_gather | solution.py:117
  121.5 3.4 fusion.112
  125.0 3.5 reduce_window_sum.23
  128.8 5.5 fusion.90
  135.8 6.2 fusion.87
  143.5 8.0 fusion.80
  152.2 3.6 collective-permute-start.1
  157.7 2.8 maximum_convert_fusion
  160.5 6.9 divide_multiply_fusion
  167.4 5.1 slice.77
  178.1 3.2 copy.64
  181.3 2.8 copy.74
  195.5 9.2 add_bitcast_fusion.1
  204.7 630.8 %custom-call.4 = f32[2,8,8,1,64,64]{4,5,3,2,1,0:T(8,128)} custom-call(f32[2,8,8,1,64,64]{5,4,3,2,1,0:T(8,128)} %add_bitcast_fusion.1), custom_call_target="InvertDiagBlocksLowerTriangular" | custom-call | tf_op jit(solution)/shard_map/jit(_solve_triangular)/vmap(vmap(vmap()))/triangular_solve | solution.py:62
  836.1 3.1 copy-done.3
  839.2 8.2 fusion.125
  850.0 11.8 fusion.14
  861.7 9.6 multiply_subtract_fusion
  871.4 7.0 fusion.35
  878.4 16.5 %fusion.49 = f32[8,2,8,128,128]{4,3,0,2,1:T(8,128)} fusion(f32[2,8,8,64,256]{4,3,2,1,0:T(8,128)S(1)} %fusion.14, f32[2,8,8,64,128]{4,3,2,1,0:T(8,128)S(1)} %bitcast.143, f32[2,8,8,64]{3,2,1,0:T(8,128)S(1)} %get-tuple-element.145), kind=kOutput, calls=%fused_computation.65 | convolution fusion | flops 1611661312 | bytes 16842752 | tf_op jit(solution)/shard_map/...td,...te->...de/dot_general | solution.py:19
  894.9 18.0 %bitcast_subtract_fusion = f32[8,2,8,128,128]{4,3,0,2,1:T(8,128)} fusion(f32[128,128]{1,0:T(8,128)S(1)} %fusion.111, f32[8,2,8]{0,2,1:T(8,128)S(1)} %exponential_bitcast_fusion, f32[2,8,8,64,256]{4,3,2,1,0:T(8,128)S(1)} %fusion.14, f32[2,8,8,64,128]{4,3,2,1,0:T(8,128)S(1)} %bitcast.144, f32[2,8,8,64]{3,2,1,0:T(8,128)S(1)} %get-tuple-element.145), kind=kOutput, calls=%fused_computation.26 | convolution fusion | flops 1615855616 | bytes 16916480 | tf_op jit(solution)/shard_map/...td,...te->...de/dot_general | solution.py:19
  913.0 54.5 %while.28 = (s32[]{:T(128)}, f32[2,8,128,128]{3,2,1,0:T(8,128)S(1)}, f32[2,8,128,128]{3,2,1,0:T(8,128)S(1)}, f32[8,2,8,128,128]{4,3,2,1,0:T(8,128)}, f32[8,2,8,1...) while((s32[]{:T(128)}, ...), condition=%wide.region_6.7_spmd.clone, body=%wide.region_5.6_spmd.clone.sunk | while | flops 806092800 | bytes 15730295 | solution.py:179
  967.5 12.0 fusion.19
  979.6 183.6 %while.27 = (s32[]{:T(128)}, f32[2,8,128,128]{3,2,1,0:T(8,128)S(1)}, f32[2,8,128,128]{3,2,1,0:T(8,128)S(1)}, f32[2,8,128,128]{3,2,1,0:T(8,128)S(1)}, s32[]{:T(128)}) while((s32[]{:T(128)}, f32[2,8,128,128]{3,2,1,0:T(8,128)S(1)}, f32[2,8,128,128]{3,2,1,0:T(8,128)S(1)}, f32[2,8,128,128]{3,2,1,0:T(8,128)S(1)}, s32[]{:T(128)}) %tuple.54), condition=%wide.region_8.9_spmd, body=%wide.region_7.8_spmd.sunk | while | flops 402915328 | bytes 8388709 | solution.py:192
  981.7 4.2 collective-permute-start
  985.9 21.9 %collective-permute-done = f32[2,8,128,128]{3,2,1,0:T(8,128)S(1)} collective-permute-done((f32[2,8,128,128]{3,2,1,0:T(8,128)}, f32[2,8,128,128]{3,2,1,0:T(8,128)S(1)}, u32[]{:S(2)}, u32[]{:S(2)}) %collective-permute-start) | collective-permute-done | bytes 1048608 | tf_op jit(solution)/shard_map/while/body/eval_jaxpr/ppermute | solution.py:15
  1009.9 4.3 collective-permute-start
  1014.3 21.0 %collective-permute-done = f32[2,8,128,128]{3,2,1,0:T(8,128)S(1)} collective-permute-done((f32[2,8,128,128]{3,2,1,0:T(8,128)}, f32[2,8,128,128]{3,2,1,0:T(8,128)S(1)}, u32[]{:S(2)}, u32[]{:S(2)}) %collective-permute-start) | collective-permute-done | bytes 1048608 | tf_op jit(solution)/shard_map/while/body/eval_jaxpr/ppermute | solution.py:15
  1037.4 5.2 collective-permute-start
  1042.6 20.1 %collective-permute-done = f32[2,8,128,128]{3,2,1,0:T(8,128)S(1)} collective-permute-done((f32[2,8,128,128]{3,2,1,0:T(8,128)}, f32[2,8,128,128]{3,2,1,0:T(8,128)S(1)}, u32[]{:S(2)}, u32[]{:S(2)}) %collective-permute-start) | collective-permute-done | bytes 1048608 | tf_op jit(solution)/shard_map/while/body/eval_jaxpr/ppermute | solution.py:15
  1064.8 5.2 collective-permute-start
  1070.1 19.1 %collective-permute-done = f32[2,8,128,128]{3,2,1,0:T(8,128)S(1)} collective-permute-done((f32[2,8,128,128]{3,2,1,0:T(8,128)}, f32[2,8,128,128]{3,2,1,0:T(8,128)S(1)}, u32[]{:S(2)}, u32[]{:S(2)}) %collective-permute-start) | collective-permute-done | bytes 1048608 | tf_op jit(solution)/shard_map/while/body/eval_jaxpr/ppermute | solution.py:15
  1091.3 5.2 collective-permute-start
  1096.6 18.2 %collective-permute-done = f32[2,8,128,128]{3,2,1,0:T(8,128)S(1)} collective-permute-done((f32[2,8,128,128]{3,2,1,0:T(8,128)}, f32[2,8,128,128]{3,2,1,0:T(8,128)S(1)}, u32[]{:S(2)}, u32[]{:S(2)}) %collective-permute-start) | collective-permute-done | bytes 1048608 | tf_op jit(solution)/shard_map/while/body/eval_jaxpr/ppermute | solution.py:15
  1116.9 5.2 collective-permute-start
  1122.2 17.3 %collective-permute-done = f32[2,8,128,128]{3,2,1,0:T(8,128)S(1)} collective-permute-done((f32[2,8,128,128]{3,2,1,0:T(8,128)}, f32[2,8,128,128]{3,2,1,0:T(8,128)S(1)}, u32[]{:S(2)}, u32[]{:S(2)}) %collective-permute-start) | collective-permute-done | bytes 1048608 | tf_op jit(solution)/shard_map/while/body/eval_jaxpr/ppermute | solution.py:15
  1141.6 5.2 collective-permute-start
  1146.8 16.4 %collective-permute-done = f32[2,8,128,128]{3,2,1,0:T(8,128)S(1)} collective-permute-done((f32[2,8,128,128]{3,2,1,0:T(8,128)}, f32[2,8,128,128]{3,2,1,0:T(8,128)S(1)}, u32[]{:S(2)}, u32[]{:S(2)}) %collective-permute-start) | collective-permute-done | bytes 1048608 | tf_op jit(solution)/shard_map/while/body/eval_jaxpr/ppermute | solution.py:15
  1163.2 5.6 fusion.97
  1168.9 11.6 multiply_reduce_fusion
  1183.3 5.1 mul.221
  1188.4 7.5 copy.53
  1195.9 4.9 reshape.107
  1200.8 17.0 %fusion.25 = f32[512,2,2048]{2,0,1:T(8,128)} fusion(bf16[1024,2048]{1,0:T(8,128)(2,1)} %param.37, f32[2,512,1024]{2,1,0:T(8,128)} %reshape.107, f32[2,512,1024]{2,1,0:T(8,128)} %mul.221, f32[1024]{0:T(1024)S(1)} %copy-done.25, bf16[2,512,2048]{2,1,0:T(8,128)(2,1)} %all-gather.2.cloned.1.call-done, bf16[2048,1024]{1,0:T(8,128)(2,1)} %param.27), kind=kOutput, calls=%fused_computation.39 | convolution fusion | flops 8600420352 | bytes 29364224 | tf_op jit(solution)/shard_map/tse,ed->tsd/dot_general | solution.py:202
  1217.8 74.6 %reduce-scatter.2.cloned.1.call-done = f32[128,2,2048]{2,0,1:T(8,128)} async-done(((f32[512,2,2048]{2,0,1:T(8,128)}), f32[128,2,2048]{2,0,1:T(8,128)}) %reduce-scatter.2.cloned.1.call-update) | async-done | bytes 2097168 | tf_op jit(solution)/shard_map/reduce_scatter | solution.py:201
  1292.4 2.7 convert_bitcast_fusion
  (159 shorter events, 105.3 us)
Async XLA Ops:
  6.5 122.2 %copy-start = (bf16[2048,512]{1,0:T(8,128)(2,1)S(1)}, bf16[2048,512]{1,0:T(8,128)(2,1)}, u32[]{:S(2)}) copy-start(bf16[2048,512]{1,0:T(8,128)(2,1)} %param.25) | copy-start | bytes 6291460
  6.5 81.1 %copy-start.29 = (f32[8]{0:T(128)S(1)}, f32[8]{0:T(128)}, u32[]{:S(2)}) copy-start(f32[8]{0:T(128)} %param.33) | copy-start | bytes 100
  6.5 81.2 %copy-start.21 = (f32[4,512]{1,0:T(4,128)S(1)}, f32[4,512]{1,0:T(4,128)}, u32[]{:S(2)}) copy-start(f32[4,512]{1,0:T(4,128)} %param.30) | copy-start | bytes 24580
  6.5 81.2 %copy-start.22 = (f32[4,512]{1,0:T(4,128)S(1)}, f32[4,512]{1,0:T(4,128)}, u32[]{:S(2)}) copy-start(f32[4,512]{1,0:T(4,128)} %param.31) | copy-start | bytes 24580
  6.5 81.2 %copy-start.20 = (f32[4,1024]{1,0:T(4,128)S(1)}, f32[4,1024]{1,0:T(4,128)}, u32[]{:S(2)}) copy-start(f32[4,1024]{1,0:T(4,128)} %param.32) | copy-start | bytes 49156
  6.5 82.4 %copy-start.28 = (f32[128]{0:T(128)S(1)}, f32[128]{0:T(128)}, u32[]{:S(2)}) copy-start(f32[128]{0:T(128)} %param.36) | copy-start | bytes 1540
  6.6 115.0 %copy-start.27 = (f32[8]{0:T(128)S(1)}, f32[8]{0:T(128)}, u32[]{:S(2)}) copy-start(f32[8]{0:T(128)} %param.34) | copy-start | bytes 100
  6.6 114.9 %copy-start.12 = (bf16[2048,8]{0,1:T(8,128)(2,1)S(1)}, bf16[2048,8]{0,1:T(8,128)(2,1)}, u32[]{:S(2)}) copy-start(bf16[2048,8]{0,1:T(8,128)(2,1)} %param.28) | copy-start | bytes 98308
  6.6 77.5 %all-reduce.2.cloned.1.call-start = ((), (), s32[]{:S(2)}) async-start(), calls=%async_computation.1 | async-start | bytes 524288 | tf_op jit(solution)/shard_map/psum | solution.py:111
  10.7 110.8 %all-gather.2.cloned.1.call-start = ((), (), s32[]{:S(2)}) async-start(), calls=%async_computation.2 | async-start | bytes 5242880 | tf_op jit(solution)/shard_map/all_gather | solution.py:117
  87.6 1204.8 %reduce-scatter.2.cloned.1.call-start = ((), (), s32[]{:S(2)}) async-start(), calls=%async_computation.3 | async-start | bytes 10485760 | tf_op jit(solution)/shard_map/reduce_scatter | solution.py:201
  143.5 12.3 copy-start.26
  151.5 5.5 copy-start.10
  151.5 4.3 copy-start.8
  151.5 4.3 copy-start.13
  152.2 5.5 collective-permute-start.1
  157.1 3.3 copy-start.14
  157.1 3.3 copy-start.15
  157.1 3.3 copy-start.16
  157.1 3.3 copy-start.17
  167.4 6.2 copy-start.7
  191.4 1.7 copy-start.11
  193.0 2.5 copy-start.18
  193.1 2.5 copy-start.19
  193.1 2.5 copy-start.23
  193.1 2.5 copy-start.24
  193.5 2.0 copy-start.2
  835.5 3.7 copy-start.3
  836.1 13.9 %copy-start.4 = (f32[2,512,4,2,128]{4,1,3,2,0:T(8,128)}, f32[2,512,4,2,128]{4,1,3,2,0:T(8,128)S(1)}, u32[]{:S(2)}) copy-start(f32[2,512,4,2,128]{4,1,3,2,0:T(8,128)S(1)} %broadcast_in_dim.30) | copy-start | bytes 12582916
  861.7 9.6 copy-start.5
  981.7 26.1 %collective-permute-start = (f32[2,8,128,128]{3,2,1,0:T(8,128)}, f32[2,8,128,128]{3,2,1,0:T(8,128)S(1)}, u32[]{:S(2)}, u32[]{:S(2)}) collective-permute-start(f32[2,8,128,128]{3,2,1,0:T(8,128)} %convolution_add_fusion.6), channel_id=1, source_target_pairs={{0,4},{4,8},{8,12},{12,16},{16,20},{20,24},{24,28},{1,5},{5,9},{9,... | collective-permute-start | bytes 3145736 | tf_op jit(solution)/shard_map/while/body/eval_jaxpr/ppermute | solution.py:15
  1009.9 25.3 %collective-permute-start = (f32[2,8,128,128]{3,2,1,0:T(8,128)}, f32[2,8,128,128]{3,2,1,0:T(8,128)S(1)}, u32[]{:S(2)}, u32[]{:S(2)}) collective-permute-start(f32[2,8,128,128]{3,2,1,0:T(8,128)} %convolution_add_fusion.6), channel_id=1, source_target_pairs={{0,4},{4,8},{8,12},{12,16},{16,20},{20,24},{24,28},{1,5},{5,9},{9,... | collective-permute-start | bytes 3145736 | tf_op jit(solution)/shard_map/while/body/eval_jaxpr/ppermute | solution.py:15
  1037.4 25.3 %collective-permute-start = (f32[2,8,128,128]{3,2,1,0:T(8,128)}, f32[2,8,128,128]{3,2,1,0:T(8,128)S(1)}, u32[]{:S(2)}, u32[]{:S(2)}) collective-permute-start(f32[2,8,128,128]{3,2,1,0:T(8,128)} %convolution_add_fusion.6), channel_id=1, source_target_pairs={{0,4},{4,8},{8,12},{12,16},{16,20},{20,24},{24,28},{1,5},{5,9},{9,... | collective-permute-start | bytes 3145736 | tf_op jit(solution)/shard_map/while/body/eval_jaxpr/ppermute | solution.py:15
  1064.8 24.4 %collective-permute-start = (f32[2,8,128,128]{3,2,1,0:T(8,128)}, f32[2,8,128,128]{3,2,1,0:T(8,128)S(1)}, u32[]{:S(2)}, u32[]{:S(2)}) collective-permute-start(f32[2,8,128,128]{3,2,1,0:T(8,128)} %convolution_add_fusion.6), channel_id=1, source_target_pairs={{0,4},{4,8},{8,12},{12,16},{16,20},{20,24},{24,28},{1,5},{5,9},{9,... | collective-permute-start | bytes 3145736 | tf_op jit(solution)/shard_map/while/body/eval_jaxpr/ppermute | solution.py:15
  1091.3 23.5 %collective-permute-start = (f32[2,8,128,128]{3,2,1,0:T(8,128)}, f32[2,8,128,128]{3,2,1,0:T(8,128)S(1)}, u32[]{:S(2)}, u32[]{:S(2)}) collective-permute-start(f32[2,8,128,128]{3,2,1,0:T(8,128)} %convolution_add_fusion.6), channel_id=1, source_target_pairs={{0,4},{4,8},{8,12},{12,16},{16,20},{20,24},{24,28},{1,5},{5,9},{9,... | collective-permute-start | bytes 3145736 | tf_op jit(solution)/shard_map/while/body/eval_jaxpr/ppermute | solution.py:15
  1116.9 22.5 %collective-permute-start = (f32[2,8,128,128]{3,2,1,0:T(8,128)}, f32[2,8,128,128]{3,2,1,0:T(8,128)S(1)}, u32[]{:S(2)}, u32[]{:S(2)}) collective-permute-start(f32[2,8,128,128]{3,2,1,0:T(8,128)} %convolution_add_fusion.6), channel_id=1, source_target_pairs={{0,4},{4,8},{8,12},{12,16},{16,20},{20,24},{24,28},{1,5},{5,9},{9,... | collective-permute-start | bytes 3145736 | tf_op jit(solution)/shard_map/while/body/eval_jaxpr/ppermute | solution.py:15
  1141.6 21.6 %collective-permute-start = (f32[2,8,128,128]{3,2,1,0:T(8,128)}, f32[2,8,128,128]{3,2,1,0:T(8,128)S(1)}, u32[]{:S(2)}, u32[]{:S(2)}) collective-permute-start(f32[2,8,128,128]{3,2,1,0:T(8,128)} %convolution_add_fusion.6), channel_id=1, source_target_pairs={{0,4},{4,8},{8,12},{12,16},{16,20},{20,24},{24,28},{1,5},{5,9},{9,... | collective-permute-start | bytes 3145736 | tf_op jit(solution)/shard_map/while/body/eval_jaxpr/ppermute | solution.py:15
  1163.2 5.6 copy-start.6
  1163.2 5.7 copy-start.9
  1195.9 4.9 copy-start.25
  1217.8 77.3 %copy-start.1 = (bf16[2048,512]{1,0:T(8,128)(2,1)S(1)}, bf16[2048,512]{1,0:T(8,128)(2,1)}, u32[]{:S(2)}) copy-start(bf16[2048,512]{1,0:T(8,128)(2,1)} %param.25) | copy-start | bytes 6291460
Sparse Core Ops, SparseCore 0:
  10.8 73.2 all-reduce.1
  87.7 33.7 all-gather.1
  1217.9 74.4 reduce-scatter.1
where the time goes:
time: 1310 us; the launch traced here: 1300 us
  other arithmetic  671 us (51%)
  waiting for transfers between devices  313 us (24%)
  matrix products  212 us (16%)
  local copies, waits for them, and re-layouts  52.8 us (4%)
  starting transfers between devices  38.4 us (3%)
  between operations  14.2 us (1%)
    another operation x3, other arithmetic, group_terms(): jax.scipy.linalg.solve_triangular(system, right_side, lower=True, unit_di...  631 us
    dot_general x34, matrix products, product(): return jnp.einsum(form, left, right, precision=HIGH)  159 us
    ppermute x8, waiting for transfers between devices, shifted(): return lax.ppermute(shard, axis, pairs)  135 us
    reduce_scatter x1, waiting for transfers between devices, per_device(): lax.psum_scatter(jnp.einsum('tse,ed->tsd', hidden, w_out, preferred_eleme...  74.6 us
    psum x1, waiting for transfers between devices, per_device(): totals = lax.psum(partial_sums, 'ctx')  73.4 us
    ppermute x8, starting transfers between devices, shifted(): return lax.ppermute(shard, axis, pairs)  38.3 us
    all_gather x1, waiting for transfers between devices, per_device(): whole = lax.all_gather(augmented, 'head', axis=2, tiled=True)  30.6 us
  transfers between devices with their start and end apart: 11, of which 11 were waited for; matrix products, arithmetic and copies ran while one was open for 0% of the time, Pallas kernels for 0%

commit v1 on v0

v1 whole, which is shorter than its diff:
```python
import jax
import jax.numpy as jnp
from jax import lax
from jax.experimental import pallas as pl
from jax.experimental.pallas import tpu as pltpu
from jax.sharding import PartitionSpec as P

CHUNK = 128
HIGH = lax.Precision.HIGHEST
BF16 = jnp.bfloat16
F32 = jnp.float32


def shifted(shard, axis, by):
    length = lax.axis_size(axis)
    pairs = [(i, i + by) for i in range(length) if 0 <= i + by < length]
    return lax.ppermute(shard, axis, pairs)


def dot(left, right):
    return jnp.dot(left.astype(BF16), right.astype(BF16), preferred_element_type=F32)


def silu(x):
    return x * (0.5 + 0.5 * jnp.tanh(0.5 * x))


def unit_inverses(lowers):
    size = lowers[0].shape[0]
    row = lax.broadcasted_iota(jnp.int32, (size, size), 0)
    col = lax.broadcasted_iota(jnp.int32, (size, size), 1)
    eye = (row == col).astype(F32)
    pair = (row // 2 == col // 2).astype(F32)
    inverses = [eye - pair * lower for lower in lowers]
    half = 2
    while half < size:
        below = ((row // (2 * half) == col // (2 * half)) & (row // half != col // half)).astype(F32)
        halves = [inverse.astype(BF16) for inverse in inverses]
        inner = [dot(lower * below, inverse) for lower, inverse in zip(lowers, halves)]
        outer = [dot(inverse, term) for inverse, term in zip(halves, inner)]
        inverses = [inverse - term for inverse, term in zip(inverses, outer)]
        half *= 2
    return inverses


def delta_kernel(
    q_ref, k_ref, v_ref, rq_ref, rk_ref, rv_ref, tq_ref, tk_ref, tv_ref, col_ref, row_ref,
    state_ref, query_ref, base_ref, scr,
):
    tok = q_ref.shape[1]
    dim = q_ref.shape[2]
    share = v_ref.shape[2] // dim
    chunks = tok // CHUNK

    def conv(raw_ref, rim_ref, taps_ref, which):
        lanes = slice(which * dim, (which + 1) * dim)
        scr[0:8, :] = rim_ref[0, :, lanes]
        scr[8 : 8 + tok, :] = raw_ref[0, :, lanes].astype(F32)
        total = taps_ref[0:1, lanes] * scr[5 : 5 + tok, :]
        for i in range(1, 4):
            total = total + taps_ref[i : i + 1, lanes] * scr[5 + i : 5 + i + tok, :]
        return silu(total)

    queries = conv(q_ref, rq_ref, tq_ref, 0)
    queries = queries * (
        lax.rsqrt(jnp.sum(queries * queries, axis=-1, keepdims=True) + 1e-06) * dim ** (-0.5)
    )
    keys = conv(k_ref, rk_ref, tk_ref, 0)
    keys = keys * lax.rsqrt(jnp.sum(keys * keys, axis=-1, keepdims=True) + 1e-06)
    values = [conv(v_ref, rv_ref, tv_ref, j) for j in range(share)]

    row = lax.broadcasted_iota(jnp.int32, (CHUNK, CHUNK), 0)
    col = lax.broadcasted_iota(jnp.int32, (CHUNK, CHUNK), 1)
    incl = row >= col
    strict = row > col
    units = [(c, j) for c in range(chunks) for j in range(share)]
    lowers, attends, rights, sides, tails, decays = [], [], [], [], [], []
    for c in range(chunks):
        span = slice(c * CHUNK, (c + 1) * CHUNK)
        qc = queries[span]
        kc = keys[span]
        both = jnp.concatenate([qc, kc], axis=0).astype(BF16)
        kt = kc.T
        gram = dot(both, kt)
        for j in range(share):
            cc = col_ref[0, 0, span, j : j + 1]
            bc = col_ref[0, 0, span, share + j : share + j + 1]
            cr = row_ref[0, 0, j : j + 1, span]
            last = row_ref[0, 0, j : j + 1, (c + 1) * CHUNK - 1 : (c + 1) * CHUNK]
            ratio = jnp.where(incl, jnp.exp(jnp.minimum(cc - cr, 0.0)), 0.0)
            lowers.append(jnp.where(strict, ratio * gram[CHUNK:] * bc, 0.0))
            scaled = jnp.exp(cc)
            rights.append(
                jnp.concatenate([bc * values[j][span], (bc * scaled) * kc], axis=1).astype(BF16)
            )
            attends.append(
                jnp.concatenate([ratio * gram[:CHUNK], jnp.exp(last - cr) * kt], axis=0).astype(BF16)
            )
            sides.append((scaled * qc).astype(BF16))
            decays.append(jnp.exp(last))
    inverses = unit_inverses(lowers)
    solved = [dot(inverse, right) for inverse, right in zip(inverses, rights)]

    eye = (row == col).astype(F32)
    zero = jnp.zeros((CHUNK, dim), F32)
    states = [jnp.concatenate([eye, zero], axis=1) for _ in range(share)]
    for c in range(chunks):
        span = slice(c * CHUNK, (c + 1) * CHUNK)
        for j in range(share):
            u = c * share + j
            local = solved[u][:, :dim]
            left = jnp.concatenate([solved[u][:, dim:].astype(BF16), sides[u]], axis=0)
            seen = dot(left, states[j])
            delta = jnp.concatenate([zero, local], axis=1) - seen[:CHUNK]
            moved = dot(attends[u], delta)
            out = seen[CHUNK:] + moved[:CHUNK]
            states[j] = decays[u] * states[j] + moved[CHUNK:]
            lanes = slice(j * dim, (j + 1) * dim)
            query_ref[0, span, lanes] = out[:, :dim].astype(BF16)
            base_ref[0, span, lanes] = out[:, dim:]
    for j in range(share):
        state_ref[0, j] = states[j].astype(BF16)


def delta_local(q, k, v, rims, taps, cols, rows, dim):
    seqs, tok, qk_width = q.shape
    groups = qk_width // dim
    share = v.shape[2] // qk_width
    wide = share * dim
    narrow = pl.BlockSpec((1, tok, dim), lambda s, g: (s, 0, g))
    broad = pl.BlockSpec((1, tok, wide), lambda s, g: (s, 0, g))
    return pl.pallas_call(
        delta_kernel,
        grid=(seqs, groups),
        in_specs=[
            narrow,
            narrow,
            broad,
            pl.BlockSpec((1, 8, dim), lambda s, g: (s, 0, g)),
            pl.BlockSpec((1, 8, dim), lambda s, g: (s, 0, g)),
            pl.BlockSpec((1, 8, wide), lambda s, g: (s, 0, g)),
            pl.BlockSpec((4, dim), lambda s, g: (0, g)),
            pl.BlockSpec((4, dim), lambda s, g: (0, g)),
            pl.BlockSpec((4, wide), lambda s, g: (0, g)),
            pl.BlockSpec((1, 1, tok, 2 * share), lambda s, g: (g, s, 0, 0)),
            pl.BlockSpec((1, 1, share, tok), lambda s, g: (g, s, 0, 0)),
        ],
        out_specs=[
            pl.BlockSpec((1, share, dim, 2 * dim), lambda s, g: (s, g, 0, 0)),
            broad,
            broad,
        ],
        out_shape=[
            jax.ShapeDtypeStruct((seqs, groups * share, dim, 2 * dim), BF16),
            jax.ShapeDtypeStruct(v.shape, BF16),
            jax.ShapeDtypeStruct(v.shape, F32),
        ],
        scratch_shapes=[pltpu.VMEM((tok + 8, dim), F32)],
        compiler_params=pltpu.CompilerParams(vmem_limit_bytes=40 << 20),
        cost_estimate=pl.CostEstimate(
            flops=40 * seqs * tok * v.shape[2] * dim, bytes_accessed=16 << 20, transcendentals=0
        ),
    )(q, k, v, *rims, *taps, cols, rows)


def prefix_kernel(maps_ref, out_ref):
    steps, chains, dim, _ = maps_ref.shape
    states = [jnp.zeros((dim, dim), F32) for _ in range(chains)]
    for step in range(steps):
        for c in range(chains):
            out_ref[step, c] = states[c].astype(BF16)
            if step < steps - 1:
                now = maps_ref[step, c, :, :dim]
                top = states[c].astype(BF16)
                rest = states[c] - top.astype(F32)
                states[c] = maps_ref[step, c, :, dim:].astype(F32) + dot(now, top) + dot(now, rest)


def prefix_states(maps):
    steps, chains, dim, _ = maps.shape
    return pl.pallas_call(
        prefix_kernel,
        out_shape=jax.ShapeDtypeStruct((steps, chains, dim, dim), BF16),
        compiler_params=pltpu.CompilerParams(vmem_limit_bytes=24 << 20),
    )(maps)


def finish_kernel(query_ref, base_ref, gate_ref, state_ref, gain_ref, out_ref):
    dim = gain_ref.shape[1]
    for j in range(out_ref.shape[1] // dim):
        lanes = slice(j * dim, (j + 1) * dim)
        out = dot(query_ref[0, :, lanes], state_ref[0, j]) + base_ref[0, :, lanes]
        mean_sq = jnp.mean(out * out, axis=-1, keepdims=True)
        gate = silu(gate_ref[0, :, lanes].astype(F32))
        out_ref[:, lanes] = (out * lax.rsqrt(mean_sq + 1e-06) * gain_ref[...] * gate).astype(BF16)


def finish(query, base, gate, states, gain, seq):
    tok, width = query.shape[1:]
    dim = gain.shape[0]
    share = 2
    wide = share * dim
    broad = pl.BlockSpec((1, tok, wide), lambda g: (seq, 0, g))
    return pl.pallas_call(
        finish_kernel,
        grid=(width // wide,),
        in_specs=[
            broad,
            broad,
            broad,
            pl.BlockSpec((1, share, dim, dim), lambda g: (seq, g, 0, 0)),
            pl.BlockSpec((1, dim), lambda g: (0, 0)),
        ],
        out_specs=pl.BlockSpec((tok, wide), lambda g: (0, g)),
        out_shape=jax.ShapeDtypeStruct((tok, width), BF16),
        compiler_params=pltpu.CompilerParams(vmem_limit_bytes=24 << 20),
    )(query, base, gate, states, gain.reshape(1, dim))


def augment(tokens, region_lengths, header_lengths):
    tok = tokens.shape[1]
    place = lax.axis_index("ctx")
    parts = lax.axis_size("ctx")
    longest = tok * parts // 16
    hops = -(-(longest - 1) // tok)
    position = place * tok + jnp.arange(tok, dtype=jnp.int32)
    ends = jnp.cumsum(region_lengths, axis=1)
    starts = ends - region_lengths
    span = jnp.minimum(header_lengths, region_lengths)
    inside = (position[None, None, :] >= starts[:, :, None]) & (
        position[None, None, :] < ends[:, :, None]
    )
    header = inside & (position[None, None, :] < (starts + span)[:, :, None])

    def holds(point):
        return ((starts <= point) & (point < ends))[:, :, None]

    sums = jnp.einsum("srt,std->srd", header.astype(BF16), tokens, preferred_element_type=F32)

    def part_at(point):
        return jnp.sum(jnp.where(holds(point), sums, 0.0), axis=1)

    before = shifted(part_at((place + 1) * tok), "ctx", 1)
    for hop in range(2, hops + 1):
        before = before + shifted(part_at((place + hop) * tok), "ctx", hop)
    after = shifted(part_at(place * tok), "ctx", -1)
    totals = (
        sums
        + jnp.where(holds(place * tok), before[:, None, :], 0.0)
        + jnp.where(holds((place + 1) * tok), after[:, None, :], 0.0)
    )
    means = totals / span[..., None].astype(F32)
    top = means.astype(BF16)
    rest = (means - top.astype(F32)).astype(BF16)
    spread = inside.astype(BF16)
    added = jnp.einsum(
        "srt,srd->std",
        jnp.concatenate([spread, spread], axis=1),
        jnp.concatenate([top, rest], axis=1),
        preferred_element_type=F32,
    )
    return (tokens.astype(F32) + added).astype(BF16)


def incoming_states(maps, dim):
    seqs, heads = maps.shape[:2]
    parts = lax.axis_size("ctx")
    chains = seqs * heads
    if chains % parts == 0:
        sent = maps.reshape(parts, chains // parts, dim, 2 * dim)
        held = lax.all_to_all(sent, "ctx", 0, 0, tiled=True)
        states = lax.all_to_all(prefix_states(held), "ctx", 0, 0, tiled=True)
        return states.reshape(seqs, heads, dim, dim)

    def relay(counter, state):
        moved = jnp.einsum(
            "shde,shef->shdf", maps[..., :dim], state, preferred_element_type=F32
        ) + maps[..., dim:].astype(F32)
        return shifted(moved.astype(BF16), "ctx", 1)

    return lax.fori_loop(0, parts - 1, relay, jnp.zeros((seqs, heads, dim, dim), BF16))


def per_device(
    tokens,
    region_lengths,
    header_lengths,
    w_query,
    w_key,
    w_value,
    w_gate,
    w_decay,
    w_beta,
    conv_query,
    conv_key,
    conv_value,
    decay_rate,
    decay_bias,
    beta_bias,
    norm_gain,
    w_out,
):
    seqs, tok, _ = tokens.shape
    dim = norm_gain.shape[0]
    heads = w_decay.shape[1]
    groups = w_query.shape[1] // dim
    share = heads // groups
    chunks = tok // CHUNK
    augmented = augment(tokens, region_lengths, header_lengths)
    whole = lax.all_gather(augmented, "head", axis=2, tiled=True)

    def project(weight):
        return jnp.einsum("std,de->ste", whole, weight, preferred_element_type=F32)

    raws = [project(weight).astype(BF16) for weight in (w_query, w_key, w_value)]
    rim = shifted(jnp.concatenate([raw[:, tok - 3 :, :] for raw in raws], axis=-1), "ctx", 1)
    gate_raw = project(w_gate).astype(BF16)
    small = project(jnp.concatenate([w_decay, w_beta], axis=1))
    log_decay = -decay_rate * jax.nn.softplus(small[..., :heads] + decay_bias)
    strength = jax.nn.sigmoid(small[..., heads:] + beta_bias)
    places = jnp.arange(CHUNK)
    below = (places[:, None] >= places[None, :]).astype(F32)
    cumul = jnp.einsum(
        "ij,scjh->scih", below, log_decay.reshape(seqs, chunks, CHUNK, heads), precision=HIGH
    ).reshape(seqs, tok, groups, share)
    strength = strength.reshape(seqs, tok, groups, share)
    cols = jnp.concatenate([cumul, strength], axis=-1).transpose(2, 0, 1, 3)
    rows = cumul.transpose(2, 0, 3, 1)
    rim = jnp.pad(rim.astype(F32), ((0, 0), (5, 0), (0, 0)))
    width = groups * dim
    rims = (rim[..., :width], rim[..., width : 2 * width], rim[..., 2 * width :])
    maps, query_total, base_total = delta_local(
        *raws, rims, (conv_query, conv_key, conv_value), cols, rows, dim
    )
    states = incoming_states(maps, dim)
    mixed = []
    for seq in range(seqs):
        hidden = finish(query_total, base_total, gate_raw, states, norm_gain, seq)
        partial = jnp.dot(hidden, w_out, preferred_element_type=F32).astype(BF16)
        mixed.append(lax.psum_scatter(partial, "head", scatter_dimension=0, tiled=True))
    return jnp.stack(mixed)


def solution(mesh):
    return jax.shard_map(
        per_device,
        mesh=mesh,
        in_specs=(
            P(None, "ctx", "head"),
            P(),
            P(),
            P(None, "head"),
            P(None, "head"),
            P(None, "head"),
            P(None, "head"),
            P(None, "head"),
            P(None, "head"),
            P(None, "head"),
            P(None, "head"),
            P(None, "head"),
            P("head"),
            P("head"),
            P("head"),
            P(),
            P("head", None),
        ),
        out_specs=P(None, ("ctx", "head"), None),
        check_vma=False,
    )
```

time: 1310 us -> 264 us (0.20)
  other arithmetic: 671 us -> 5.79 us
  waiting for transfers between devices: 313 us -> 97 us
  matrix products: 212 us -> 39.8 us
  Pallas kernels: 0 us -> 42.4 us
  local copies, waits for them, and re-layouts: 52.8 us -> 20 us
  blocking collectives: 0 us -> 31.2 us
  starting transfers between devices: 38.4 us -> 13.7 us
    another operation x7 -> x2, other arithmetic: 636 us -> 3.32 us  [the longest x1 2.27 us: per_device(): return jnp.stack(mixed)]
    dot_general x40 -> x10, matrix products: 200 us -> 39.8 us  [the longest x5 27.7 us: project(): return jnp.einsum('std,de->ste', whole, weight, preferred_element_type=F32)]
    ppermute x8 -> x3, waiting for transfers between devices: 135 us -> 4.77 us  [shifted(): return lax.ppermute(shard, axis, pairs)]
    psum x1 -> x0, waiting for transfers between devices: 73.4 us -> none  [per_device(): totals = lax.psum(partial_sums, 'ctx')]
    pallas_call x0 -> x4, Pallas kernels: none -> 42.4 us  [the longest x1 36 us: delta_local(): pl.pallas_call(delta_kernel, grid=(seqs, groups), in_specs=[narrow, narro...]
    all_to_all x0 -> x1, blocking collectives: none -> 31.2 us  [incoming_states(): held = lax.all_to_all(sent, 'ctx', 0, 0, tiled=True)]
    ppermute x8 -> x3, starting transfers between devices: 38.3 us -> 9.82 us  [shifted(): return lax.ppermute(shard, axis, pairs)]
    reduce_scatter x1 -> x2, waiting for transfers between devices: 74.6 us -> 51.7 us  [per_device(): lax.psum_scatter(partial, 'head', scatter_dimension=0, tiled=True)]
  transfers between devices with their start and end apart: 11 -> 7, of which waited for: 11 -> 6; matrix products, arithmetic and copies ran while one was open for 0% -> 5% of each run, Pallas kernels for 0% -> 1%
where the time goes in v1:
time: 264 us; the launch traced here: 263 us
  waiting for transfers between devices  97 us (37%)
  Pallas kernels  42.4 us (16%)
  matrix products  39.8 us (15%)
  blocking collectives  31.2 us (12%)
  local copies, waits for them, and re-layouts  20 us (8%)
  starting transfers between devices  13.7 us (5%)
  between operations  13.5 us (5%)
  other arithmetic  5.79 us (2%)
    reduce_scatter x2, waiting for transfers between devices, per_device(): lax.psum_scatter(partial, 'head', scatter_dimension=0, tiled=True)  51.7 us
    pallas_call x1, Pallas kernels, delta_local(): pl.pallas_call(delta_kernel, grid=(seqs, groups), in_specs=[narrow, narro...  36 us
    all_gather x1, waiting for transfers between devices, per_device(): whole = lax.all_gather(augmented, 'head', axis=2, tiled=True)  35.8 us
    all_to_all x1, blocking collectives, incoming_states(): held = lax.all_to_all(sent, 'ctx', 0, 0, tiled=True)  31.2 us
    dot_general x5, matrix products, project(): return jnp.einsum('std,de->ste', whole, weight, preferred_element_type=F32)  27.7 us
    unnamed x52, local copies, waits for them, and re-layouts  15.8 us
    ppermute x3, starting transfers between devices, shifted(): return lax.ppermute(shard, axis, pairs)  9.82 us
    dot_general x2, matrix products, per_device(): partial = jnp.dot(hidden, w_out, preferred_element_type=F32).astype(BF16)  7.37 us
  transfers between devices with their start and end apart: 7, of which 6 were waited for; matrix products, arithmetic and copies ran while one was open for 5% of the time, Pallas kernels for 1%

profile of v1, /device:TPU:0, one launch (start us, length us, event | category | flops | bytes accessed | tf_op | source)
XLA Modules:
  0.0 263.3 jit_solution(13394540685657844315)
XLA Ops:
  6.5 0.0 all-gather.2.cloned.1.call-start
  6.6 1.1 reduce_window_sum.11
  7.7 0.7 compare_and_fusion.2
  8.3 0.7 minimum_add_fusion
  9.0 1.7 select_reduce_fusion.1
  10.8 4.8 %collective-permute-start = (f32[2,512]{1,0:T(2,128)S(1)}, f32[2,512]{1,0:T(2,128)S(1)}, u32[]{:S(2)}, u32[]{:S(2)}) collective-permute-start(f32[2,512]{1,0:T(2,128)S(1)} %get-tuple-element.11), channel_id=1, source_target_pairs={{0,4},{4,8},{8,12},{12,16},{16,20},{20,24},{24,28},{1,5},{5,9},{9,... | collective-permute-start | bytes 12296 | tf_op jit(solution)/shard_map/ppermute | solution.py:17
  15.6 1.3 collective-permute-start.1
  16.9 0.2 compare_and_fusion
  17.1 4.0 %collective-permute-done.1 = f32[2,512]{1,0:T(2,128)S(1)} collective-permute-done((f32[2,512]{1,0:T(2,128)S(1)}, f32[2,512]{1,0:T(2,128)S(1)}, u32[]{:S(2)}, u32[]{:S(2)}) %collective-permute-start.1) | collective-permute-done | bytes 4128 | tf_op jit(solution)/shard_map/ppermute | solution.py:17
  21.1 0.1 fusion.36
  21.3 2.7 %add_convert_fusion = bf16[2,512,512]{2,1,0:T(8,128)(2,1)} fusion(bf16[2,512,512]{2,1,0:T(8,128)(2,1)} %param.17, pred[2,64,512]{1,2,0:T(32,128)(4,1)S(1)} %compare_and_fusion, bf16[2,64,512]{2,1,0:T(8,128)(2,1)S(1)} %get-tuple-element.16, bf16[2,64,512]{2,1,0:T(8,128)(2,1)S(1)} %get-tuple-element.15), kind=kOutput, calls=%fused_computation.11 | convolution fusion | flops 136445952 | bytes 2424832 | tf_op jit(solution)/shard_map/srt,srd->std/dot_general | solution.py:256
  24.0 35.8 %all-gather.2.cloned.1.call-done = bf16[2,512,2048]{2,1,0:T(8,128)(2,1)} async-done(((bf16[2,512,512]{2,1,0:T(8,128)(2,1)}), bf16[2,512,2048]{2,1,0:T(8,128)(2,1)}) %all-gather.2.cloned.1.call-update) | async-done | bytes 4194320 | tf_op jit(solution)/shard_map/all_gather | solution.py:310
  59.8 3.4 %fusion.31 = f32[2,512,16]{1,2,0:T(8,128)S(1)} fusion(bf16[2,512,2048]{2,1,0:T(8,128)(2,1)} %all-gather.2.cloned.1.call-done, bf16[2048,8]{0,1:T(8,128)(2,1)S(1)} %copy-done.18, bf16[2048,8]{0,1:T(8,128)(2,1)S(1)} %copy-done.19), kind=kOutput, calls=%fused_computation.36 | convolution fusion | flops 67239936 | bytes 4325376 | tf_op jit(solution)/shard_map/std,de->ste/dot_general | solution.py:313
  63.2 0.1 fusion.43
  63.3 0.2 convolution_bitcast_fusion
  63.7 4.7 %fusion.17.k_ref = bf16[2,512,512]{2,1,0:T(8,128)(2,1)S(1)} fusion(bf16[2,512,2048]{2,1,0:T(8,128)(2,1)} %all-gather.2.cloned.1.call-done, bf16[2048,512]{1,0:T(8,128)(2,1)S(1)} %copy-done), kind=kOutput, calls=%fused_computation.15 | convolution fusion | flops 2148007936 | bytes 7340032 | tf_op jit(solution)/shard_map/std,de->ste/dot_general | solution.py:313
  68.4 2.3 fusion.14.q_ref
  70.7 1.0 copy-done.10
  71.7 2.0 copy.35
  73.8 2.0 copy.36
  75.8 8.1 %fusion.8.v_ref = bf16[2,512,1024]{2,1,0:T(8,128)(2,1)S(1)} fusion(bf16[2,512,2048]{2,1,0:T(8,128)(2,1)} %all-gather.2.cloned.1.call-done, bf16[2048,1024]{1,0:T(8,128)(2,1)} %param.22), kind=kOutput, calls=%fused_computation.12 | convolution fusion | flops 4296015872 | bytes 10485760 | tf_op jit(solution)/shard_map/std,de->ste/dot_general | solution.py:313
  84.0 3.7 %collective-permute-start.2 = (bf16[2,3,2048]{2,1,0:T(4,128)(2,1)S(1)}, bf16[2,3,2048]{2,1,0:T(4,128)(2,1)S(1)}, u32[]{:S(2)}, u32[]{:S(2)}) collective-permute-start(bf16[2,3,2048]{2,1,0:T(4,128)(2,1)S(1)} %pad_maximum_fusion.1), channel_id=1, source_target_pairs={{0,4},{4,8},{8,12},{12,16},{16,20},{20,24},{24,28},{1,5},{5,9},{9,... | collective-permute-start | bytes 73736 | tf_op jit(solution)/shard_map/ppermute | solution.py:17
  87.7 0.6 maximum_bitcast_fusion.col_ref
  88.3 0.8 collective-permute-done.2
  89.1 36.0 %shard_map.163 = (bf16[2,8,128,256]{3,2,1,0:T(8,128)(2,1)S(1)}, bf16[2,512,1024]{2,1,0:T(8,128)(2,1)S(1)}, f32[2,512,1024]{2,1,0:T(8,128)S(1)}) custom-call(bf16[2,512,512]{2,1,0:T(8,128)(2,1)S(1)} %copy-done.11, bf16[2,512,512]{2,1,0:T(8,128)(2,1)S(1)} %fusion.17.k_ref, bf16[2,512,1024]{2,1,0:T(8,128)(2,1)S(1)} %fusion.8.v_ref, ...), custom_call_target="tpu_custom_call" | custom-call | flops 5368709120 | bytes 16777216 | tf_op jit(solution)/shard_map/pallas_call | solution.py:132
  125.1 2.0 copy-done.1
  127.1 1.4 copy-done.4
  128.5 31.2 %all_to_all.10.maps_ref = bf16[8,2,128,256]{3,2,1,0:T(8,128)(2,1)S(1)} all-to-all(bf16[8,2,128,256]{3,2,1,0:T(8,128)(2,1)S(1)} %bitcast.58), channel_id=1, replica_groups=mesh['ctx'=8,'head'=4] {'ctx'}, dimensions={0} | all-to-all | bytes 2097152 | tf_op jit(solution)/shard_map/all_to_all | solution.py:271
  159.7 1.9 shard_map.164
  161.6 3.5 %all-to-all-start.1 = ((bf16[8,2,128,128]{3,2,1,0:T(8,128)(2,1)}), bf16[8,2,128,128]{3,2,1,0:T(8,128)(2,1)S(1)}, u32[]{:S(2)}, u32[]{:S(2)}) async-start(bf16[8,2,128,128]{3,2,1,0:T(8,128)(2,1)} %shard_map.164), calls=%async_computation.1 | async-start | bytes 1048576 | tf_op jit(solution)/shard_map/all_to_all | solution.py:272
  165.2 0.0 reduce-scatter.3.cloned.1.call-start
  165.2 9.3 %fusion.11.gate_ref = bf16[2,512,1024]{2,1,0:T(8,128)(2,1)} fusion(bf16[2,512,2048]{2,1,0:T(8,128)(2,1)} %all-gather.2.cloned.1.call-done, bf16[2048,1024]{1,0:T(8,128)(2,1)} %param.23), kind=kOutput, calls=%fused_computation.13 | convolution fusion | flops 4296015872 | bytes 10485760 | tf_op jit(solution)/shard_map/std,de->ste/dot_general | solution.py:313
  174.5 4.7 %all-to-all-done.1 = bf16[8,2,128,128]{3,2,1,0:T(8,128)(2,1)S(1)} async-done(((bf16[8,2,128,128]{3,2,1,0:T(8,128)(2,1)}), bf16[8,2,128,128]{3,2,1,0:T(8,128)(2,1)S(1)}, u32[]{:S(2)}, u32[]{:S(2)}) %all-to-all-start.1) | async-done | bytes 524320 | tf_op jit(solution)/shard_map/all_to_all | solution.py:272
  179.2 2.2 copy-done.2
  181.4 1.6 copy-done.5
  183.0 1.6 copy-done.7
  184.6 2.2 shard_map.165
  186.9 3.7 %convolution_convert_fusion.1 = bf16[512,2048]{1,0:T(8,128)(2,1)} fusion(bf16[512,1024]{1,0:T(8,128)(2,1)S(1)} %shard_map.165, bf16[1024,2048]{1,0:T(8,128)(2,1)S(1)} %copy-done.21), kind=kOutput, calls=%fused_computation.5 | convolution fusion | flops 2148532224 | bytes 7340032 | tf_op jit(solution)/shard_map/dot_general | solution.py:339
  190.6 0.3 reduce-scatter.5.cloned.1.call-start
  190.9 2.2 copy-done.3
  193.0 1.9 copy-done.6
  194.9 1.8 copy-done.8
  196.7 2.2 shard_map.166
  199.0 0.1 copy-done.22
  199.1 3.7 %convolution_convert_fusion = bf16[512,2048]{1,0:T(8,128)(2,1)} fusion(bf16[512,1024]{1,0:T(8,128)(2,1)S(1)} %shard_map.166, bf16[1024,2048]{1,0:T(8,128)(2,1)S(1)} %copy-done.22), kind=kOutput, calls=%fused_computation.4 | convolution fusion | flops 2148532224 | bytes 7340032 | tf_op jit(solution)/shard_map/dot_general | solution.py:339
  202.8 17.5 %reduce-scatter.3.cloned.1.call-done = bf16[128,2048]{1,0:T(8,128)(2,1)} async-done(((bf16[512,2048]{1,0:T(8,128)(2,1)}), bf16[128,2048]{1,0:T(8,128)(2,1)}) %reduce-scatter.3.cloned.1.call-update) | async-done | bytes 524304 | tf_op jit(solution)/shard_map/reduce_scatter | solution.py:340
  220.3 34.2 %reduce-scatter.5.cloned.1.call-done = bf16[128,2048]{1,0:T(8,128)(2,1)} async-done(((bf16[512,2048]{1,0:T(8,128)(2,1)}), bf16[128,2048]{1,0:T(8,128)(2,1)}) %reduce-scatter.5.cloned.1.call-update) | async-done | bytes 524304 | tf_op jit(solution)/shard_map/reduce_scatter | solution.py:340
  254.5 2.3 pad_maximum_fusion
  (59 shorter events, 0.3 us)
Async XLA Ops:
  6.5 57.1 %copy-start = (bf16[2048,512]{1,0:T(8,128)(2,1)S(1)}, bf16[2048,512]{1,0:T(8,128)(2,1)}, u32[]{:S(2)}) copy-start(bf16[2048,512]{1,0:T(8,128)(2,1)} %param.21) | copy-start | bytes 6291460
  6.5 17.4 %copy-start.24 = (f32[8]{0:T(128)S(1)}, f32[8]{0:T(128)}, u32[]{:S(2)}) copy-start(f32[8]{0:T(128)} %param.29) | copy-start | bytes 100
  6.5 53.3 %copy-start.18 = (bf16[2048,8]{0,1:T(8,128)(2,1)S(1)}, bf16[2048,8]{0,1:T(8,128)(2,1)}, u32[]{:S(2)}) copy-start(bf16[2048,8]{0,1:T(8,128)(2,1)} %param.25) | copy-start | bytes 98308
  6.5 53.3 %copy-start.19 = (bf16[2048,8]{0,1:T(8,128)(2,1)S(1)}, bf16[2048,8]{0,1:T(8,128)(2,1)}, u32[]{:S(2)}) copy-start(bf16[2048,8]{0,1:T(8,128)(2,1)} %param.24) | copy-start | bytes 98308
  6.5 53.3 %all-gather.2.cloned.1.call-start = ((), (), s32[]{:S(2)}) async-start(), calls=%async_computation.4 | async-start | bytes 5242880 | tf_op jit(solution)/shard_map/all_gather | solution.py:310
  10.8 6.3 %collective-permute-start = (f32[2,512]{1,0:T(2,128)S(1)}, f32[2,512]{1,0:T(2,128)S(1)}, u32[]{:S(2)}, u32[]{:S(2)}) collective-permute-start(f32[2,512]{1,0:T(2,128)S(1)} %get-tuple-element.11), channel_id=1, source_target_pairs={{0,4},{4,8},{8,12},{12,16},{16,20},{20,24},{24,28},{1,5},{5,9},{9,... | collective-permute-start | bytes 12296 | tf_op jit(solution)/shard_map/ppermute | solution.py:17
  15.6 5.5 %collective-permute-start.1 = (f32[2,512]{1,0:T(2,128)S(1)}, f32[2,512]{1,0:T(2,128)S(1)}, u32[]{:S(2)}, u32[]{:S(2)}) collective-permute-start(f32[2,512]{1,0:T(2,128)S(1)} %get-tuple-element.12), channel_id=1, source_target_pairs={{4,0},{8,4},{12,8},{16,12},{20,16},{24,20},{28,24},{5,1},{9,5},{13... | collective-permute-start | bytes 12296 | tf_op jit(solution)/shard_map/ppermute | solution.py:17
  21.1 42.1 %copy-start.20 = (f32[8]{0:T(128)S(1)}, f32[8]{0:T(128)}, u32[]{:S(2)}) copy-start(f32[8]{0:T(128)} %param.31) | copy-start | bytes 100
  21.1 42.2 %copy-start.25 = (f32[8]{0:T(128)S(1)}, f32[8]{0:T(128)}, u32[]{:S(2)}) copy-start(f32[8]{0:T(128)} %param.30) | copy-start | bytes 100
  63.7 4.7 %copy-start.17 = (bf16[2,512,2048]{2,1,0:T(8,128)(2,1)S(1)}, bf16[2,512,2048]{2,1,0:T(8,128)(2,1)}, u32[]{:S(2)}) copy-start(bf16[2,512,2048]{2,1,0:T(8,128)(2,1)} %all-gather.2.cloned.1.call-done) | copy-start | bytes 12582916
  63.7 4.7 %copy-start.23 = (bf16[2048,512]{1,0:T(8,128)(2,1)S(1)}, bf16[2048,512]{1,0:T(8,128)(2,1)}, u32[]{:S(2)}) copy-start(bf16[2048,512]{1,0:T(8,128)(2,1)} %param.20) | copy-start | bytes 6291460
  70.7 1.0 copy-start.10
  75.8 11.9 %copy-start.15 = (f32[2,512,4,2]{3,1,0,2:T(8,128)S(1)}, f32[2,512,4,2]{3,1,0,2:T(8,128)}, u32[]{:S(2)}) copy-start(f32[2,512,4,2]{3,1,0,2:T(8,128)} %copy.35) | copy-start | bytes 98308
  75.8 11.9 %copy-start.16 = (f32[2,512,4,2]{3,1,0,2:T(8,128)S(1)}, f32[2,512,4,2]{3,1,0,2:T(8,128)}, u32[]{:S(2)}) copy-start(f32[2,512,4,2]{3,1,0,2:T(8,128)} %copy.36) | copy-start | bytes 98308
  83.9 5.2 %copy-start.11 = (bf16[2,512,512]{2,1,0:T(8,128)(2,1)S(1)}, bf16[2,512,512]{2,1,0:T(8,128)(2,1)}, u32[]{:S(2)}) copy-start(bf16[2,512,512]{2,1,0:T(8,128)(2,1)} %copy-done.10) | copy-start | bytes 3145732
  83.9 5.2 %copy-start.12 = (f32[4,1024]{1,0:T(4,128)S(1)}, f32[4,1024]{1,0:T(4,128)}, u32[]{:S(2)}) copy-start(f32[4,1024]{1,0:T(4,128)} %tv_ref.1) | copy-start | bytes 49156
  83.9 5.2 %copy-start.13 = (f32[4,512]{1,0:T(4,128)S(1)}, f32[4,512]{1,0:T(4,128)}, u32[]{:S(2)}) copy-start(f32[4,512]{1,0:T(4,128)} %tq_ref.1) | copy-start | bytes 24580
  83.9 5.2 %copy-start.14 = (f32[4,512]{1,0:T(4,128)S(1)}, f32[4,512]{1,0:T(4,128)}, u32[]{:S(2)}) copy-start(f32[4,512]{1,0:T(4,128)} %tk_ref.1) | copy-start | bytes 24580
  84.0 5.1 %collective-permute-start.2 = (bf16[2,3,2048]{2,1,0:T(4,128)(2,1)S(1)}, bf16[2,3,2048]{2,1,0:T(4,128)(2,1)S(1)}, u32[]{:S(2)}, u32[]{:S(2)}) collective-permute-start(bf16[2,3,2048]{2,1,0:T(4,128)(2,1)S(1)} %pad_maximum_fusion.1), channel_id=1, source_target_pairs={{0,4},{4,8},{8,12},{12,16},{16,20},{20,24},{24,28},{1,5},{5,9},{9,... | collective-permute-start | bytes 73736 | tf_op jit(solution)/shard_map/ppermute | solution.py:17
  125.1 2.0 copy-start.1
  127.1 1.4 copy-start.4
  161.6 17.6 %all-to-all-start.1 = ((bf16[8,2,128,128]{3,2,1,0:T(8,128)(2,1)}), bf16[8,2,128,128]{3,2,1,0:T(8,128)(2,1)S(1)}, u32[]{:S(2)}, u32[]{:S(2)}) async-start(bf16[8,2,128,128]{3,2,1,0:T(8,128)(2,1)} %shard_map.164), calls=%async_computation.1 | async-start | bytes 1048576 | tf_op jit(solution)/shard_map/all_to_all | solution.py:272
  165.2 14.0 %copy-start.9 = (f32[128]{0:T(128)S(1)}, f32[128]{0:T(128)}, u32[]{:S(2)}) copy-start(f32[128]{0:T(128)} %param.32) | copy-start | bytes 1540
  165.2 55.1 %reduce-scatter.3.cloned.1.call-start = ((), (), s32[]{:S(2)}) async-start(), calls=%async_computation.5 | async-start | bytes 2621440 | tf_op jit(solution)/shard_map/reduce_scatter | solution.py:340
  179.2 2.2 copy-start.2
  181.4 1.6 copy-start.5
  183.0 1.6 copy-start.7
  184.6 2.2 copy-start.21
  190.6 63.9 %reduce-scatter.5.cloned.1.call-start = ((), (), s32[]{:S(2)}) async-start(), calls=%async_computation.6 | async-start | bytes 2621440 | tf_op jit(solution)/shard_map/reduce_scatter | solution.py:340
  190.8 2.2 copy-start.3
  193.0 1.9 copy-start.6
  194.9 1.8 copy-start.8
  196.7 2.4 copy-start.22
Sparse Core Ops, SparseCore 0:
  24.1 35.6 all-gather.1
  190.7 29.5 reduce-scatter.2
  223.0 31.4 reduce-scatter.4

commit v2 on v1

v2 whole, which is shorter than its diff:
```python
import jax
import jax.numpy as jnp
from jax import lax
from jax.experimental import pallas as pl
from jax.experimental.pallas import tpu as pltpu
from jax.sharding import PartitionSpec as P

CHUNK = 128
HIGH = lax.Precision.HIGHEST
BF16 = jnp.bfloat16
F32 = jnp.float32


def shifted(shard, axis, by):
    length = lax.axis_size(axis)
    pairs = [(i, i + by) for i in range(length) if 0 <= i + by < length]
    return lax.ppermute(shard, axis, pairs)


def dot(left, right):
    return jnp.dot(left.astype(BF16), right.astype(BF16), preferred_element_type=F32)


def silu(x):
    return x * (0.5 + 0.5 * jnp.tanh(0.5 * x))


def unit_inverses(lowers):
    size = lowers[0].shape[0]
    row = lax.broadcasted_iota(jnp.int32, (size, size), 0)
    col = lax.broadcasted_iota(jnp.int32, (size, size), 1)
    eye = (row == col).astype(F32)
    pair = (row // 2 == col // 2).astype(F32)
    inverses = [eye - pair * lower for lower in lowers]
    half = 2
    while half < size:
        below = ((row // (2 * half) == col // (2 * half)) & (row // half != col // half)).astype(F32)
        halves = [inverse.astype(BF16) for inverse in inverses]
        inner = [dot(lower * below, inverse) for lower, inverse in zip(lowers, halves)]
        outer = [dot(inverse, term) for inverse, term in zip(halves, inner)]
        inverses = [inverse - term for inverse, term in zip(inverses, outer)]
        half *= 2
    return inverses


def delta_kernel(
    q_ref, k_ref, v_ref, rq_ref, rk_ref, rv_ref, tq_ref, tk_ref, tv_ref, col_ref, row_ref,
    state_ref, query_ref, base_ref, scr,
):
    tok, dim = q_ref.shape
    share = v_ref.shape[1] // dim
    chunks = tok // CHUNK

    def conv(raw_ref, rim_ref, taps_ref, which):
        lanes = slice(which * dim, (which + 1) * dim)
        scr[0:8, :] = rim_ref[:, lanes]
        scr[8 : 8 + tok, :] = raw_ref[:, lanes].astype(F32)
        total = taps_ref[0:1, lanes] * scr[5 : 5 + tok, :]
        for i in range(1, 4):
            total = total + taps_ref[i : i + 1, lanes] * scr[5 + i : 5 + i + tok, :]
        return silu(total)

    queries = conv(q_ref, rq_ref, tq_ref, 0)
    queries = queries * (
        lax.rsqrt(jnp.sum(queries * queries, axis=-1, keepdims=True) + 1e-06) * dim ** (-0.5)
    )
    keys = conv(k_ref, rk_ref, tk_ref, 0)
    keys = keys * lax.rsqrt(jnp.sum(keys * keys, axis=-1, keepdims=True) + 1e-06)
    values = [conv(v_ref, rv_ref, tv_ref, j) for j in range(share)]

    row = lax.broadcasted_iota(jnp.int32, (CHUNK, CHUNK), 0)
    col = lax.broadcasted_iota(jnp.int32, (CHUNK, CHUNK), 1)
    incl = row >= col
    strict = row > col
    units = [(c, j) for c in range(chunks) for j in range(share)]
    lowers, attends, rights, sides, tails, decays = [], [], [], [], [], []
    for c in range(chunks):
        span = slice(c * CHUNK, (c + 1) * CHUNK)
        qc = queries[span]
        kc = keys[span]
        both = jnp.concatenate([qc, kc], axis=0).astype(BF16)
        kt = kc.T
        gram = dot(both, kt)
        for j in range(share):
            cc = col_ref[0, span, j : j + 1]
            bc = col_ref[0, span, share + j : share + j + 1]
            cr = row_ref[0, j : j + 1, span]
            last = row_ref[0, j : j + 1, (c + 1) * CHUNK - 1 : (c + 1) * CHUNK]
            ratio = jnp.where(incl, jnp.exp(jnp.minimum(cc - cr, 0.0)), 0.0)
            lowers.append(jnp.where(strict, ratio * gram[CHUNK:] * bc, 0.0))
            scaled = jnp.exp(cc)
            rights.append(
                jnp.concatenate([bc * values[j][span], (bc * scaled) * kc], axis=1).astype(BF16)
            )
            attends.append(
                jnp.concatenate([ratio * gram[:CHUNK], jnp.exp(last - cr) * kt], axis=0).astype(BF16)
            )
            sides.append((scaled * qc).astype(BF16))
            decays.append(jnp.exp(last))
    inverses = unit_inverses(lowers)
    solved = [dot(inverse, right) for inverse, right in zip(inverses, rights)]

    eye = (row == col).astype(F32)
    zero = jnp.zeros((CHUNK, dim), F32)
    states = [jnp.concatenate([eye, zero], axis=1) for _ in range(share)]
    for c in range(chunks):
        span = slice(c * CHUNK, (c + 1) * CHUNK)
        for j in range(share):
            u = c * share + j
            local = solved[u][:, :dim]
            left = jnp.concatenate([solved[u][:, dim:].astype(BF16), sides[u]], axis=0)
            seen = dot(left, states[j])
            delta = jnp.concatenate([zero, local], axis=1) - seen[:CHUNK]
            moved = dot(attends[u], delta)
            out = seen[CHUNK:] + moved[:CHUNK]
            states[j] = decays[u] * states[j] + moved[CHUNK:]
            lanes = slice(j * dim, (j + 1) * dim)
            query_ref[span, lanes] = out[:, :dim].astype(BF16)
            base_ref[span, lanes] = out[:, dim:]
    for j in range(share):
        state_ref[j] = states[j].astype(BF16)


def delta_local(q, k, v, rims, taps, cols, rows, dim):
    tok, qk_width = q.shape
    groups = qk_width // dim
    share = v.shape[1] // qk_width
    wide = share * dim
    narrow = pl.BlockSpec((tok, dim), lambda g: (0, g))
    broad = pl.BlockSpec((tok, wide), lambda g: (0, g))
    return pl.pallas_call(
        delta_kernel,
        grid=(groups,),
        in_specs=[
            narrow,
            narrow,
            broad,
            pl.BlockSpec((8, dim), lambda g: (0, g)),
            pl.BlockSpec((8, dim), lambda g: (0, g)),
            pl.BlockSpec((8, wide), lambda g: (0, g)),
            pl.BlockSpec((4, dim), lambda g: (0, g)),
            pl.BlockSpec((4, dim), lambda g: (0, g)),
            pl.BlockSpec((4, wide), lambda g: (0, g)),
            pl.BlockSpec((1, tok, 2 * share), lambda g: (g, 0, 0)),
            pl.BlockSpec((1, share, tok), lambda g: (g, 0, 0)),
        ],
        out_specs=[
            pl.BlockSpec((share, dim, 2 * dim), lambda g: (g, 0, 0)),
            broad,
            broad,
        ],
        out_shape=[
            jax.ShapeDtypeStruct((groups * share, dim, 2 * dim), BF16),
            jax.ShapeDtypeStruct(v.shape, BF16),
            jax.ShapeDtypeStruct(v.shape, F32),
        ],
        scratch_shapes=[pltpu.VMEM((tok + 8, dim), F32)],
        compiler_params=pltpu.CompilerParams(vmem_limit_bytes=48 << 20),
        cost_estimate=pl.CostEstimate(
            flops=300 * tok * v.shape[1] * dim, bytes_accessed=8 << 20, transcendentals=0
        ),
    )(q, k, v, *rims, *taps, cols, rows)


def prefix_kernel(maps_ref, out_ref):
    steps, chains, dim, _ = maps_ref.shape
    states = [jnp.zeros((dim, dim), F32) for _ in range(chains)]
    for step in range(steps):
        for c in range(chains):
            out_ref[step, c] = states[c].astype(BF16)
            if step < steps - 1:
                now = maps_ref[step, c, :, :dim]
                top = states[c].astype(BF16)
                rest = states[c] - top.astype(F32)
                states[c] = maps_ref[step, c, :, dim:].astype(F32) + dot(now, top) + dot(now, rest)


def prefix_states(maps):
    steps, chains, dim, _ = maps.shape
    return pl.pallas_call(
        prefix_kernel,
        out_shape=jax.ShapeDtypeStruct((steps, chains, dim, dim), BF16),
        compiler_params=pltpu.CompilerParams(vmem_limit_bytes=24 << 20),
    )(maps)


def finish_kernel(query_ref, base_ref, gate_ref, state_ref, gain_ref, out_ref):
    dim = gain_ref.shape[1]
    for j in range(out_ref.shape[1] // dim):
        lanes = slice(j * dim, (j + 1) * dim)
        out = dot(query_ref[:, lanes], state_ref[j]) + base_ref[:, lanes]
        mean_sq = jnp.mean(out * out, axis=-1, keepdims=True)
        gate = silu(gate_ref[:, lanes].astype(F32))
        out_ref[:, lanes] = (out * lax.rsqrt(mean_sq + 1e-06) * gain_ref[...] * gate).astype(BF16)


def finish(query, base, gate, states, gain):
    tok, width = query.shape
    dim = gain.shape[0]
    share = 2
    wide = share * dim
    broad = pl.BlockSpec((tok, wide), lambda g: (0, g))
    return pl.pallas_call(
        finish_kernel,
        grid=(width // wide,),
        in_specs=[
            broad,
            broad,
            broad,
            pl.BlockSpec((share, dim, dim), lambda g: (g, 0, 0)),
            pl.BlockSpec((1, dim), lambda g: (0, 0)),
        ],
        out_specs=broad,
        out_shape=jax.ShapeDtypeStruct((tok, width), BF16),
        compiler_params=pltpu.CompilerParams(vmem_limit_bytes=48 << 20),
        cost_estimate=pl.CostEstimate(flops=1 << 31, bytes_accessed=8 << 20, transcendentals=0),
    )(query, base, gate, states, gain.reshape(1, dim))


def augment(tokens, lengths, headers):
    tok = tokens.shape[0]
    place = lax.axis_index("ctx")
    parts = lax.axis_size("ctx")
    longest = tok * parts // 16
    hops = -(-(longest - 1) // tok)
    position = place * tok + jnp.arange(tok, dtype=jnp.int32)
    ends = jnp.cumsum(lengths)
    starts = ends - lengths
    span = jnp.minimum(headers, lengths)
    inside = (position[None, :] >= starts[:, None]) & (position[None, :] < ends[:, None])
    header = inside & (position[None, :] < (starts + span)[:, None])

    def holds(point):
        return ((starts <= point) & (point < ends))[:, None]

    sums = jnp.einsum("rt,td->rd", header.astype(BF16), tokens, preferred_element_type=F32)

    def part_at(point):
        return jnp.sum(jnp.where(holds(point), sums, 0.0), axis=0, keepdims=True)

    before = shifted(part_at((place + 1) * tok), "ctx", 1)
    for hop in range(2, hops + 1):
        before = before + shifted(part_at((place + hop) * tok), "ctx", hop)
    after = shifted(part_at(place * tok), "ctx", -1)
    totals = (
        sums
        + jnp.where(holds(place * tok), before, 0.0)
        + jnp.where(holds((place + 1) * tok), after, 0.0)
    )
    means = totals / span[:, None].astype(F32)
    top = means.astype(BF16)
    rest = (means - top.astype(F32)).astype(BF16)
    spread = inside.astype(BF16)
    added = jnp.einsum(
        "rt,rd->td",
        jnp.concatenate([spread, spread], axis=0),
        jnp.concatenate([top, rest], axis=0),
        preferred_element_type=F32,
    )
    return (tokens.astype(F32) + added).astype(BF16)


def incoming_states(maps, dim):
    heads = maps.shape[0]
    parts = lax.axis_size("ctx")
    if heads % parts == 0:
        sent = maps.reshape(parts, heads // parts, dim, 2 * dim)
        held = lax.all_to_all(sent, "ctx", 0, 0, tiled=True)
        states = lax.all_to_all(prefix_states(held), "ctx", 0, 0, tiled=True)
        return states.reshape(heads, dim, dim)

    def relay(counter, state):
        moved = jnp.einsum(
            "hde,hef->hdf", maps[..., :dim], state, preferred_element_type=F32
        ) + maps[..., dim:].astype(F32)
        return shifted(moved.astype(BF16), "ctx", 1)

    return lax.fori_loop(0, parts - 1, relay, jnp.zeros((heads, dim, dim), BF16))


def head_sum(hidden, w_out):
    size = lax.axis_size("head")
    me = lax.axis_index("head")
    chips = size // 2
    core, chip = me % 2, me // 2
    rows = hidden.shape[0] // size
    cut = hidden.reshape(chips, 2, rows, hidden.shape[1])

    def half(which):
        picked = lax.dynamic_index_in_dim(cut, which, 1, keepdims=False)
        return jnp.dot(
            picked.reshape(chips * rows, hidden.shape[1]), w_out, preferred_element_type=F32
        ).astype(BF16)

    arrived = lax.ppermute(half(1 - core), "head", [(i, i ^ 1) for i in range(size)])
    both = half(core).astype(F32) + arrived.astype(F32)
    both = both.reshape(chips, rows, w_out.shape[1])
    total = lax.dynamic_index_in_dim(both, chip, 0, keepdims=False)
    for step in range(1, chips):
        leaving = lax.dynamic_index_in_dim(both, (chip + step) % chips, 0, keepdims=False)
        pairs = [(i, (i + 2 * step) % size) for i in range(size)]
        total = total + lax.ppermute(leaving.astype(BF16), "head", pairs).astype(F32)
    return total.astype(BF16)


def per_device(
    tokens,
    region_lengths,
    header_lengths,
    w_query,
    w_key,
    w_value,
    w_gate,
    w_decay,
    w_beta,
    conv_query,
    conv_key,
    conv_value,
    decay_rate,
    decay_bias,
    beta_bias,
    norm_gain,
    w_out,
):
    seqs, tok, _ = tokens.shape
    dim = norm_gain.shape[0]
    heads = w_decay.shape[1]
    groups = w_query.shape[1] // dim
    share = heads // groups
    chunks = tok // CHUNK
    width = groups * dim
    w_small = jnp.concatenate([w_decay, w_beta], axis=1)
    places = jnp.arange(CHUNK)
    below = (places[:, None] >= places[None, :]).astype(F32)

    def one(seq, earlier):
        raw = lax.all_gather(tokens[seq], "head", axis=1, tiled=True)
        if earlier is not None:
            raw, _ = lax.optimization_barrier((raw, earlier))
        whole = augment(raw, region_lengths[seq], header_lengths[seq])

        def project(weight):
            return jnp.dot(whole, weight, preferred_element_type=F32)

        raws = [project(weight).astype(BF16) for weight in (w_query, w_key, w_value)]
        rim = shifted(jnp.concatenate([raw[tok - 3 :, :] for raw in raws], axis=-1), "ctx", 1)
        gate_raw = project(w_gate).astype(BF16)
        small = project(w_small)
        log_decay = -decay_rate * jax.nn.softplus(small[:, :heads] + decay_bias)
        strength = jax.nn.sigmoid(small[:, heads:] + beta_bias)
        cumul = jnp.einsum(
            "ij,cjh->cih", below, log_decay.reshape(chunks, CHUNK, heads), precision=HIGH
        ).reshape(tok, groups, share)
        strength = strength.reshape(tok, groups, share)
        cols = jnp.concatenate([cumul, strength], axis=-1).transpose(1, 0, 2)
        rows = cumul.transpose(1, 2, 0)
        rim = jnp.pad(rim.astype(F32), ((5, 0), (0, 0)))
        rims = (rim[:, :width], rim[:, width : 2 * width], rim[:, 2 * width :])
        maps, query_total, base_total = delta_local(
            *raws, rims, (conv_query, conv_key, conv_value), cols, rows, dim
        )
        states = incoming_states(maps, dim)
        hidden = finish(query_total, base_total, gate_raw, states, norm_gain)
        return head_sum(hidden, w_out), maps

    mixed, earlier = [], None
    for seq in range(seqs):
        result, earlier = one(seq, earlier)
        mixed.append(result)
    return jnp.stack(mixed)


def solution(mesh):
    return jax.shard_map(
        per_device,
        mesh=mesh,
        in_specs=(
            P(None, "ctx", "head"),
            P(),
            P(),
            P(None, "head"),
            P(None, "head"),
            P(None, "head"),
            P(None, "head"),
            P(None, "head"),
            P(None, "head"),
            P(None, "head"),
            P(None, "head"),
            P(None, "head"),
            P("head"),
            P("head"),
            P("head"),
            P(),
            P("head", None),
        ),
        out_specs=P(None, ("ctx", "head"), None),
        check_vma=False,
    )
```

time: 264 us -> 240 us (0.909)
  waiting for transfers between devices: 97 us -> 56.2 us
  blocking collectives: 31.2 us -> 0 us
  starting transfers between devices: 13.7 us -> 43.3 us
  local copies, waits for them, and re-layouts: 20 us -> 27.5 us
  matrix products: 39.8 us -> 47.1 us
  Pallas kernels: 42.4 us -> 46.1 us
    reduce_scatter x2 -> x0, waiting for transfers between devices: 51.7 us -> none  [per_device(): lax.psum_scatter(partial, 'head', scatter_dimension=0, tiled=True)]
    all_to_all x1 -> x0, blocking collectives: 31.2 us -> none  [incoming_states(): held = lax.all_to_all(sent, 'ctx', 0, 0, tiled=True)]
    ppermute x0 -> x4, waiting for transfers between devices: none -> 17.5 us  [the longest x2 17.3 us: head_sum(): lax.ppermute(leaving.astype(BF16), 'head', pairs).astype(F32)]
    all_to_all x0 -> x2, starting transfers between devices: none -> 12.9 us  [incoming_states(): held = lax.all_to_all(sent, 'ctx', 0, 0, tiled=True)]
    all_gather x1 -> x2, waiting for transfers between devices: 35.8 us -> 23.8 us  [one(): raw = lax.all_gather(tokens[seq], 'head', axis=1, tiled=True)]
    ppermute x3 -> x6, starting transfers between devices: 9.82 us -> 18.4 us  [shifted(): return lax.ppermute(shard, axis, pairs)]
    all_to_all x0 -> x2, waiting for transfers between devices: none -> 8.55 us  [incoming_states(): held = lax.all_to_all(sent, 'ctx', 0, 0, tiled=True)]
    dot_general x10 -> x20, matrix products: 39.8 us -> 47.1 us  [the longest x10 28.2 us: project(): return jnp.dot(whole, weight, preferred_element_type=F32)]
  transfers between devices with their start and end apart: 7 -> 16, of which waited for: 6 -> 8; matrix products, arithmetic and copies ran while one was open for 5% -> 21% of each run, Pallas kernels for 1% -> 18%
where the time goes in v2:
time: 240 us; the launch traced here: 238 us
  waiting for transfers between devices  56.2 us (23%)
  matrix products  47.1 us (20%)
  Pallas kernels  46.1 us (19%)
  starting transfers between devices  43.3 us (18%)
  local copies, waits for them, and re-layouts  27.5 us (11%)
  between operations  14.1 us (6%)
  other arithmetic  3.8 us (2%)
    pallas_call x2, Pallas kernels, delta_local(): pl.pallas_call(delta_kernel, grid=(groups,), in_specs=[narrow, narrow, br...  37 us
    dot_general x10, matrix products, project(): return jnp.dot(whole, weight, preferred_element_type=F32)  28.2 us
    all_gather x2, waiting for transfers between devices, one(): raw = lax.all_gather(tokens[seq], 'head', axis=1, tiled=True)  23.8 us
    unnamed x89, local copies, waits for them, and re-layouts  18.7 us
    ppermute x6, starting transfers between devices, shifted(): return lax.ppermute(shard, axis, pairs)  18.4 us
    ppermute x2, waiting for transfers between devices, head_sum(): lax.ppermute(leaving.astype(BF16), 'head', pairs).astype(F32)  17.3 us
    all_to_all x2, starting transfers between devices, incoming_states(): held = lax.all_to_all(sent, 'ctx', 0, 0, tiled=True)  12.9 us
    dot_general x4, matrix products, half(): jnp.dot(picked.reshape(chips * rows, hidden.shape[1]), w_out, preferred_e...  10.9 us
  transfers between devices with their start and end apart: 16, of which 8 were waited for; matrix products, arithmetic and copies ran while one was open for 21% of the time, Pallas kernels for 18%

profile of v2, /device:TPU:0, one launch (start us, length us, event | category | flops | bytes accessed | tf_op | source)
XLA Modules:
  0.0 238.2 jit_solution(13733443888863033458)
XLA Ops:
  6.6 2.4 fusion.80
  10.6 23.8 %all-gather.5.cloned.1.call-done = bf16[1,512,2048]{2,1,0:T(8,128)(2,1)} async-done(((bf16[1,512,512]{2,1,0:T(8,128)(2,1)}), bf16[1,512,2048]{2,1,0:T(8,128)(2,1)}) %all-gather.5.cloned.1.call-update) | async-done | bytes 2097168 | tf_op jit(solution)/shard_map/all_gather | solution.py:337
  34.5 2.3 select_reduce_fusion.3
  36.7 3.4 %collective-permute-start = (f32[1,2048]{1,0:T(1,128)S(1)}, f32[1,2048]{1,0:T(1,128)S(1)}, u32[]{:S(2)}, u32[]{:S(2)}) collective-permute-start(f32[1,2048]{1,0:T(1,128)S(1)} %bitcast.162), channel_id=1, source_target_pairs={{0,4},{4,8},{8,12},{12,16},{16,20},{20,24},{24,28},{1,5},{5,9},{9,... | collective-permute-start | bytes 24584 | tf_op jit(solution)/shard_map/ppermute | solution.py:17
  40.1 1.3 collective-permute-start.1
  41.5 4.2 %collective-permute-done.1 = f32[1,2048]{1,0:T(1,128)S(1)} collective-permute-done((f32[1,2048]{1,0:T(1,128)S(1)}, f32[1,2048]{1,0:T(1,128)S(1)}, u32[]{:S(2)}, u32[]{:S(2)}) %collective-permute-start.1) | collective-permute-done | bytes 8224 | tf_op jit(solution)/shard_map/ppermute | solution.py:17
  48.2 5.3 %convolution_convert_fusion.7.v_ref = bf16[512,1024]{1,0:T(8,128)(2,1)S(1)} fusion(bf16[512,2048]{1,0:T(8,128)(2,1)} %copy-done.23, bf16[2048,1024]{1,0:T(8,128)(2,1)} %param.22), kind=kOutput, calls=%fused_computation.15 | convolution fusion | flops 2148007936 | bytes 7340032 | tf_op jit(solution)/shard_map/dot_general | solution.py:343
  53.5 1.2 convolution_convert_fusion.11.q_ref
  55.5 1.3 convolution_convert_fusion.10.k_ref
  57.6 4.3 %collective-permute-start.2 = (bf16[3,2048]{1,0:T(4,128)(2,1)S(1)}, bf16[3,2048]{1,0:T(4,128)(2,1)S(1)}, u32[]{:S(2)}, u32[]{:S(2)}) collective-permute-start(bf16[3,2048]{1,0:T(4,128)(2,1)S(1)} %pad_maximum_fusion.1), channel_id=1, source_target_pairs={{0,4},{4,8},{8,12},{12,16},{16,20},{20,24},{24,28},{1,5},{5,9},{9,... | collective-permute-start | bytes 36872 | tf_op jit(solution)/shard_map/ppermute | solution.py:17
  63.4 1.2 copy-done.5
  66.7 18.6 %shard_map.163 = (bf16[8,128,256]{2,1,0:T(8,128)(2,1)}, bf16[512,1024]{1,0:T(8,128)(2,1)S(1)}, f32[512,1024]{1,0:T(8,128)}) custom-call(bf16[512,512]{1,0:T(8,128)(2,1)S(1)} %copy-done.8, bf16[512,512]{1,0:T(8,128)(2,1)S(1)} %copy-done.10, bf16[512,1024]{1,0:T(8,128)(2,1)S(1)} %copy-done.5, f32[8,512]{1,0:T(8,128)S(1)} %get-tuple-element.40.rq_ref, ...), custom_call_target="tpu_custom_call" | custom-call | flops 20132659200 | bytes 8388608 | tf_op jit(solution)/shard_map/pallas_call | solution.py:131
  86.3 2.1 select_reduce_fusion.1
  88.4 4.2 %collective-permute-start.5 = (f32[1,2048]{1,0:T(1,128)S(1)}, f32[1,2048]{1,0:T(1,128)S(1)}, u32[]{:S(2)}, u32[]{:S(2)}) collective-permute-start(f32[1,2048]{1,0:T(1,128)S(1)} %bitcast.161), channel_id=1, source_target_pairs={{0,4},{4,8},{8,12},{12,16},{16,20},{20,24},{24,28},{1,5},{5,9},{9,... | collective-permute-start | bytes 24584 | tf_op jit(solution)/shard_map/ppermute | solution.py:17
  92.6 1.3 collective-permute-start.6
  93.9 6.7 %all-to-all-start = ((bf16[8,1,128,256]{3,2,1,0:T(8,128)(2,1)}), bf16[8,1,128,256]{3,2,1,0:T(8,128)(2,1)S(1)}, u32[]{:S(2)}, u32[]{:S(2)}) async-start(bf16[8,1,128,256]{3,2,1,0:T(8,128)(2,1)} %bitcast.13), calls=%async_computation | async-start | bytes 1048576 | tf_op jit(solution)/shard_map/all_to_all | solution.py:268
  100.8 2.5 %add_convert_fusion = bf16[512,2048]{1,0:T(8,128)(2,1)S(1)} fusion(bf16[512,2048]{1,0:T(8,128)(2,1)} %bitcast.146, bf16[64,2048]{1,0:T(8,128)(2,1)S(1)} %get-tuple-element.23, bf16[64,2048]{1,0:T(8,128)(2,1)S(1)} %get-tuple-element.24, pred[64,512]{1,0:T(32,128)(4,1)S(1)} %get-tuple-element.41), kind=kOutput, calls=%fused_computation | convolution fusion | flops 272695296 | bytes 4751360 | tf_op jit(solution)/shard_map/rt,rd->td/dot_general | solution.py:254
  104.3 3.3 %convolution_convert_fusion.5.v_ref = bf16[512,1024]{1,0:T(8,128)(2,1)} fusion(bf16[512,2048]{1,0:T(8,128)(2,1)S(1)} %add_convert_fusion, bf16[2048,1024]{1,0:T(8,128)(2,1)S(1)} %copy-done.37), kind=kOutput, calls=%fused_computation.13 | convolution fusion | flops 2148007936 | bytes 7340032 | tf_op jit(solution)/shard_map/dot_general | solution.py:343
  107.6 1.2 convolution_convert_fusion.9.q_ref
  109.2 2.1 convolution_convert_fusion.8.k_ref
  112.8 3.9 %collective-permute-start.7 = (bf16[3,2048]{1,0:T(4,128)(2,1)S(1)}, bf16[3,2048]{1,0:T(4,128)(2,1)S(1)}, u32[]{:S(2)}, u32[]{:S(2)}) collective-permute-start(bf16[3,2048]{1,0:T(4,128)(2,1)S(1)} %pad_maximum_fusion.2), channel_id=1, source_target_pairs={{0,4},{4,8},{8,12},{12,16},{16,20},{20,24},{24,28},{1,5},{5,9},{9,... | collective-permute-start | bytes 36872 | tf_op jit(solution)/shard_map/ppermute | solution.py:17
  116.8 1.4 copy.39.col_ref
  118.2 1.2 copy-done.1
  119.4 1.2 copy-done.3
  121.7 18.4 %shard_map.166 = (bf16[8,128,256]{2,1,0:T(8,128)(2,1)S(1)}, bf16[512,1024]{1,0:T(8,128)(2,1)S(1)}, f32[512,1024]{1,0:T(8,128)}) custom-call(bf16[512,512]{1,0:T(8,128)(2,1)S(1)} %convolution_convert_fusion.9.q_ref, bf16[512,512]{1,0:T(8,128)(2,1)S(1)} %copy-done.6, bf16[512,1024]{1,0:T(8,128)(2,1)S(1)} %copy-done.3, f32[8,512]{1,0:T(8,128)S(1)} %get-tuple-element.38.rq_ref, ...), custom_call_target="tpu_custom_call" | custom-call | flops 20132659200 | bytes 8388608 | tf_op jit(solution)/shard_map/pallas_call | solution.py:131
  141.9 6.3 %all-to-all-start.2 = ((bf16[8,1,128,256]{3,2,1,0:T(8,128)(2,1)}), bf16[8,1,128,256]{3,2,1,0:T(8,128)(2,1)S(1)}, u32[]{:S(2)}, u32[]{:S(2)}) async-start(bf16[8,1,128,256]{3,2,1,0:T(8,128)(2,1)} %bitcast.139), calls=%async_computation.2 | async-start | bytes 1048576 | tf_op jit(solution)/shard_map/all_to_all | solution.py:268
  148.2 1.7 shard_map.164
  149.9 8.5 %all-to-all-done.2.maps_ref = bf16[8,1,128,256]{3,2,1,0:T(8,128)(2,1)S(1)} async-done(((bf16[8,1,128,256]{3,2,1,0:T(8,128)(2,1)}), bf16[8,1,128,256]{3,2,1,0:T(8,128)(2,1)S(1)}, u32[]{:S(2)}, u32[]{:S(2)}) %all-to-all-start.2) | async-done | bytes 524320 | tf_op jit(solution)/shard_map/all_to_all | solution.py:268
  158.5 3.7 %all-to-all-start.1 = ((bf16[8,1,128,128]{3,2,1,0:T(8,128)(2,1)}), bf16[8,1,128,128]{3,2,1,0:T(8,128)(2,1)S(1)}, u32[]{:S(2)}, u32[]{:S(2)}) async-start(bf16[8,1,128,128]{3,2,1,0:T(8,128)(2,1)} %shard_map.164), calls=%async_computation.1 | async-start | bytes 524288 | tf_op jit(solution)/shard_map/all_to_all | solution.py:269
  162.2 6.1 %convolution_convert_fusion.6.gate_ref = bf16[512,1024]{1,0:T(8,128)(2,1)} fusion(bf16[512,2048]{1,0:T(8,128)(2,1)} %copy-done.23, bf16[2048,1024]{1,0:T(8,128)(2,1)} %param.23), kind=kOutput, calls=%fused_computation.14 | convolution fusion | flops 2148007936 | bytes 7340032 | tf_op jit(solution)/shard_map/dot_general | solution.py:343
  168.3 1.7 shard_map.167
  170.4 5.7 %all-to-all-start.3 = ((bf16[8,1,128,128]{3,2,1,0:T(8,128)(2,1)}), bf16[8,1,128,128]{3,2,1,0:T(8,128)(2,1)}, u32[]{:S(2)}, u32[]{:S(2)}) async-start(bf16[8,1,128,128]{3,2,1,0:T(8,128)(2,1)} %shard_map.167), calls=%async_computation.3 | async-start | bytes 524288 | tf_op jit(solution)/shard_map/all_to_all | solution.py:269
  176.1 6.3 %convolution_convert_fusion.4.gate_ref = bf16[512,1024]{1,0:T(8,128)(2,1)} fusion(bf16[512,2048]{1,0:T(8,128)(2,1)} %copy-done.25, bf16[2048,1024]{1,0:T(8,128)(2,1)} %param.23), kind=kOutput, calls=%fused_computation.12 | convolution fusion | flops 2148007936 | bytes 7340032 | tf_op jit(solution)/shard_map/dot_general | solution.py:343
  182.4 2.3 shard_map.165
  184.7 1.6 copy-done.16
  186.3 1.2 copy-done.20
  187.5 1.2 copy-done.22
  188.8 3.4 %shard_map.168 = bf16[512,1024]{1,0:T(8,128)(2,1)S(1)} custom-call(bf16[512,1024]{1,0:T(8,128)(2,1)S(1)} %copy-done.20, f32[512,1024]{1,0:T(8,128)S(1)} %copy-done.16, bf16[512,1024]{1,0:T(8,128)(2,1)S(1)} %copy-done.22, bf16[8,128,128]{2,1,0:T(8,128)(2,1)} %bitcast.36.state_ref, f32[1,128]{1,0:T(1,128)S(1)} %bitcast.144), custom_call_target="tpu_custom_call" | custom-call | flops 2147483648 | bytes 8388608 | tf_op jit(solution)/shard_map/pallas_call | solution.py:203
  193.3 1.4 copy-done.38
  194.7 2.2 convolution_convert_fusion.2
  196.9 2.2 convolution_convert_fusion
  199.9 3.9 %convert_add_fusion.1 = f32[256,2048]{1,0:T(8,128)S(1)} fusion(bf16[256,2048]{1,0:T(8,128)(2,1)} %collective-permute-done.3, bf16[256,1024]{1,0:T(8,128)(2,1)S(1)} %bitcast.152, bf16[1024,2048]{1,0:T(8,128)(2,1)} %param.33), kind=kOutput, calls=%fused_computation.11 | convolution fusion | flops 1075838976 | bytes 7864320 | tf_op jit(solution)/shard_map/dot_general | solution.py:291
  205.3 2.5 %convert_add_fusion = f32[256,2048]{1,0:T(8,128)S(1)} fusion(bf16[256,2048]{1,0:T(8,128)(2,1)} %collective-permute-done.8, bf16[256,1024]{1,0:T(8,128)(2,1)S(1)} %bitcast.151, bf16[1024,2048]{1,0:T(8,128)(2,1)S(1)} %copy-done.39), kind=kOutput, calls=%fused_computation.10 | convolution fusion | flops 1075838976 | bytes 7864320 | tf_op jit(solution)/shard_map/dot_general | solution.py:291
  207.9 1.4 copy-done.28
  210.1 1.5 collective-permute-start.9
  211.6 8.2 %collective-permute-done.4 = bf16[128,2048]{1,0:T(8,128)(2,1)S(1)} collective-permute-done((bf16[128,2048]{1,0:T(8,128)(2,1)}, bf16[128,2048]{1,0:T(8,128)(2,1)S(1)}, u32[]{:S(2)}, u32[]{:S(2)}) %collective-permute-start.4) | collective-permute-done | bytes 524320 | tf_op jit(solution)/shard_map/ppermute | solution.py:302
  219.8 1.3 fusion.8
  221.1 9.1 %collective-permute-done.9 = bf16[128,2048]{1,0:T(8,128)(2,1)S(1)} collective-permute-done((bf16[128,2048]{1,0:T(8,128)(2,1)}, bf16[128,2048]{1,0:T(8,128)(2,1)S(1)}, u32[]{:S(2)}, u32[]{:S(2)}) %collective-permute-start.9) | collective-permute-done | bytes 524320 | tf_op jit(solution)/shard_map/ppermute | solution.py:302
  (149 shorter events, 21.8 us)
Async XLA Ops:
  6.5 47.0 %copy-start = (bf16[2048,512]{1,0:T(8,128)(2,1)S(1)}, bf16[2048,512]{1,0:T(8,128)(2,1)}, u32[]{:S(2)}) copy-start(bf16[2048,512]{1,0:T(8,128)(2,1)} %param.20) | copy-start | bytes 6291460
  6.5 3.2 %copy-start.34 = (s32[2,64]{1,0:T(2,128)S(1)}, s32[2,64]{1,0:T(2,128)}, u32[]{:S(2)}) copy-start(s32[2,64]{1,0:T(2,128)} %param.18) | copy-start | bytes 1540
  6.5 3.9 %copy-start.36 = (s32[2,64]{1,0:T(2,128)S(1)}, s32[2,64]{1,0:T(2,128)}, u32[]{:S(2)}) copy-start(s32[2,64]{1,0:T(2,128)} %param.19) | copy-start | bytes 1540
  6.5 4.1 %copy-start.32 = (bf16[2048,8]{0,1:T(8,128)(2,1)S(1)}, bf16[2048,8]{0,1:T(8,128)(2,1)}, u32[]{:S(2)}) copy-start(bf16[2048,8]{0,1:T(8,128)(2,1)} %param.24) | copy-start | bytes 98308
  6.5 4.1 %copy-start.33 = (bf16[2048,8]{0,1:T(8,128)(2,1)S(1)}, bf16[2048,8]{0,1:T(8,128)(2,1)}, u32[]{:S(2)}) copy-start(bf16[2048,8]{0,1:T(8,128)(2,1)} %param.25) | copy-start | bytes 98308
  6.5 27.9 %all-gather.5.cloned.1.call-start = ((), (), s32[]{:S(2)}) async-start(), calls=%async_computation.4 | async-start | bytes 2621440 | tf_op jit(solution)/shard_map/all_gather | solution.py:337
  9.0 32.5 %copy-start.42 = (f32[8]{0:T(128)S(1)}, f32[8]{0:T(128)}, u32[]{:S(2)}) copy-start(f32[8]{0:T(128)} %param.29) | copy-start | bytes 100
  9.0 77.3 %all-gather.7.cloned.1.call-start = ((), (), s32[]{:S(2)}) async-start(), calls=%async_computation.5 | async-start | bytes 2621440 | tf_op jit(solution)/shard_map/all_gather | solution.py:337
  34.5 11.4 %copy-start.26 = (bf16[1,512,2048]{2,1,0:T(8,128)(2,1)S(1)}, bf16[1,512,2048]{2,1,0:T(8,128)(2,1)}, u32[]{:S(2)}) copy-start(bf16[1,512,2048]{2,1,0:T(8,128)(2,1)} %all-gather.5.cloned.1.call-done) | copy-start | bytes 6291460
  36.7 4.7 %collective-permute-start = (f32[1,2048]{1,0:T(1,128)S(1)}, f32[1,2048]{1,0:T(1,128)S(1)}, u32[]{:S(2)}, u32[]{:S(2)}) collective-permute-start(f32[1,2048]{1,0:T(1,128)S(1)} %bitcast.162), channel_id=1, source_target_pairs={{0,4},{4,8},{8,12},{12,16},{16,20},{20,24},{24,28},{1,5},{5,9},{9,... | collective-permute-start | bytes 24584 | tf_op jit(solution)/shard_map/ppermute | solution.py:17
  40.1 5.5 %collective-permute-start.1 = (f32[1,2048]{1,0:T(1,128)S(1)}, f32[1,2048]{1,0:T(1,128)S(1)}, u32[]{:S(2)}, u32[]{:S(2)}) collective-permute-start(f32[1,2048]{1,0:T(1,128)S(1)} %bitcast.159), channel_id=1, source_target_pairs={{4,0},{8,4},{12,8},{16,12},{20,16},{24,20},{28,24},{5,1},{9,5},{13... | collective-permute-start | bytes 24584 | tf_op jit(solution)/shard_map/ppermute | solution.py:17
  46.7 1.3 copy-start.23
  46.7 1.4 copy-start.35
  48.1 5.4 %copy-start.24 = (bf16[512,2048]{1,0:T(8,128)(2,1)S(1)}, bf16[512,2048]{1,0:T(8,128)(2,1)}, u32[]{:S(2)}) copy-start(bf16[512,2048]{1,0:T(8,128)(2,1)} %copy-done.23) | copy-start | bytes 6291460
  53.5 1.3 copy-start.4
  53.5 2.0 copy-start.40
  54.8 2.0 copy-start.7
  55.5 7.9 %copy-start.11 = (f32[4,1024]{1,0:T(4,128)S(1)}, f32[4,1024]{1,0:T(4,128)}, u32[]{:S(2)}) copy-start(f32[4,1024]{1,0:T(4,128)} %tv_ref.3) | copy-start | bytes 49156
  55.5 7.9 %copy-start.12 = (f32[4,512]{1,0:T(4,128)S(1)}, f32[4,512]{1,0:T(4,128)}, u32[]{:S(2)}) copy-start(f32[4,512]{1,0:T(4,128)} %tq_ref.3) | copy-start | bytes 24580
  55.5 7.9 %copy-start.13 = (f32[4,512]{1,0:T(4,128)S(1)}, f32[4,512]{1,0:T(4,128)}, u32[]{:S(2)}) copy-start(f32[4,512]{1,0:T(4,128)} %tk_ref.3) | copy-start | bytes 24580
  57.6 5.8 %collective-permute-start.2 = (bf16[3,2048]{1,0:T(4,128)(2,1)S(1)}, bf16[3,2048]{1,0:T(4,128)(2,1)S(1)}, u32[]{:S(2)}, u32[]{:S(2)}) collective-permute-start(bf16[3,2048]{1,0:T(4,128)(2,1)S(1)} %pad_maximum_fusion.1), channel_id=1, source_target_pairs={{0,4},{4,8},{8,12},{12,16},{16,20},{20,24},{24,28},{1,5},{5,9},{9,... | collective-permute-start | bytes 36872 | tf_op jit(solution)/shard_map/ppermute | solution.py:17
  63.4 1.2 copy-start.5
  88.4 12.2 %collective-permute-start.5 = (f32[1,2048]{1,0:T(1,128)S(1)}, f32[1,2048]{1,0:T(1,128)S(1)}, u32[]{:S(2)}, u32[]{:S(2)}) collective-permute-start(f32[1,2048]{1,0:T(1,128)S(1)} %bitcast.161), channel_id=1, source_target_pairs={{0,4},{4,8},{8,12},{12,16},{16,20},{20,24},{24,28},{1,5},{5,9},{9,... | collective-permute-start | bytes 24584 | tf_op jit(solution)/shard_map/ppermute | solution.py:17
  92.6 8.0 %collective-permute-start.6 = (f32[1,2048]{1,0:T(1,128)S(1)}, f32[1,2048]{1,0:T(1,128)S(1)}, u32[]{:S(2)}, u32[]{:S(2)}) collective-permute-start(f32[1,2048]{1,0:T(1,128)S(1)} %bitcast.157), channel_id=1, source_target_pairs={{4,0},{8,4},{12,8},{16,12},{20,16},{24,20},{28,24},{5,1},{9,5},{13... | collective-permute-start | bytes 24584 | tf_op jit(solution)/shard_map/ppermute | solution.py:17
  93.9 48.0 %all-to-all-start = ((bf16[8,1,128,256]{3,2,1,0:T(8,128)(2,1)}), bf16[8,1,128,256]{3,2,1,0:T(8,128)(2,1)S(1)}, u32[]{:S(2)}, u32[]{:S(2)}) async-start(bf16[8,1,128,256]{3,2,1,0:T(8,128)(2,1)} %bitcast.13), calls=%async_computation | async-start | bytes 1048576 | tf_op jit(solution)/shard_map/all_to_all | solution.py:268
  100.8 3.5 %copy-start.37 = (bf16[2048,1024]{1,0:T(8,128)(2,1)S(1)}, bf16[2048,1024]{1,0:T(8,128)(2,1)}, u32[]{:S(2)}) copy-start(bf16[2048,1024]{1,0:T(8,128)(2,1)} %param.22) | copy-start | bytes 12582916
  103.3 5.6 %copy-start.25 = (bf16[512,2048]{1,0:T(8,128)(2,1)}, bf16[512,2048]{1,0:T(8,128)(2,1)S(1)}, u32[]{:S(2)}) copy-start(bf16[512,2048]{1,0:T(8,128)(2,1)S(1)} %add_convert_fusion) | copy-start | bytes 6291460
  107.6 1.6 copy-start.41
  112.8 5.4 %collective-permute-start.7 = (bf16[3,2048]{1,0:T(4,128)(2,1)S(1)}, bf16[3,2048]{1,0:T(4,128)(2,1)S(1)}, u32[]{:S(2)}, u32[]{:S(2)}) collective-permute-start(bf16[3,2048]{1,0:T(4,128)(2,1)S(1)} %pad_maximum_fusion.2), channel_id=1, source_target_pairs={{0,4},{4,8},{8,12},{12,16},{16,20},{20,24},{24,28},{1,5},{5,9},{9,... | collective-permute-start | bytes 36872 | tf_op jit(solution)/shard_map/ppermute | solution.py:17
  141.9 16.6 %all-to-all-start.2 = ((bf16[8,1,128,256]{3,2,1,0:T(8,128)(2,1)}), bf16[8,1,128,256]{3,2,1,0:T(8,128)(2,1)S(1)}, u32[]{:S(2)}, u32[]{:S(2)}) async-start(bf16[8,1,128,256]{3,2,1,0:T(8,128)(2,1)} %bitcast.139), calls=%async_computation.2 | async-start | bytes 1048576 | tf_op jit(solution)/shard_map/all_to_all | solution.py:268
  158.5 11.9 %all-to-all-start.1 = ((bf16[8,1,128,128]{3,2,1,0:T(8,128)(2,1)}), bf16[8,1,128,128]{3,2,1,0:T(8,128)(2,1)S(1)}, u32[]{:S(2)}, u32[]{:S(2)}) async-start(bf16[8,1,128,128]{3,2,1,0:T(8,128)(2,1)} %shard_map.164), calls=%async_computation.1 | async-start | bytes 524288 | tf_op jit(solution)/shard_map/all_to_all | solution.py:269
  170.4 14.3 %all-to-all-start.3 = ((bf16[8,1,128,128]{3,2,1,0:T(8,128)(2,1)}), bf16[8,1,128,128]{3,2,1,0:T(8,128)(2,1)}, u32[]{:S(2)}, u32[]{:S(2)}) async-start(bf16[8,1,128,128]{3,2,1,0:T(8,128)(2,1)} %shard_map.167), calls=%async_computation.3 | async-start | bytes 524288 | tf_op jit(solution)/shard_map/all_to_all | solution.py:269
  176.1 6.4 %copy-start.14 = (f32[128]{0:T(128)S(1)}, f32[128]{0:T(128)}, u32[]{:S(2)}) copy-start(f32[128]{0:T(128)} %param.32) | copy-start | bytes 1540
  176.1 6.4 %copy-start.15 = (f32[512,1024]{1,0:T(8,128)S(1)}, f32[512,1024]{1,0:T(8,128)}, u32[]{:S(2)}) copy-start(f32[512,1024]{1,0:T(8,128)} %get-tuple-element.13.base_ref) | copy-start | bytes 6291460
  176.1 6.4 %copy-start.18 = (bf16[512,1024]{1,0:T(8,128)(2,1)S(1)}, bf16[512,1024]{1,0:T(8,128)(2,1)}, u32[]{:S(2)}) copy-start(bf16[512,1024]{1,0:T(8,128)(2,1)} %copy-done.17) | copy-start | bytes 3145732
  176.1 6.4 %copy-start.21 = (bf16[512,1024]{1,0:T(8,128)(2,1)S(1)}, bf16[512,1024]{1,0:T(8,128)(2,1)}, u32[]{:S(2)}) copy-start(bf16[512,1024]{1,0:T(8,128)(2,1)} %convolution_convert_fusion.6.gate_ref) | copy-start | bytes 3145732
  184.7 1.6 copy-start.16
  192.1 2.6 %copy-start.38 = (bf16[1024,2048]{1,0:T(8,128)(2,1)S(1)}, bf16[1024,2048]{1,0:T(8,128)(2,1)}, u32[]{:S(2)}) copy-start(bf16[1024,2048]{1,0:T(8,128)(2,1)} %param.33) | copy-start | bytes 12582916
  196.9 3.0 %collective-permute-start.3 = (bf16[256,2048]{1,0:T(8,128)(2,1)}, bf16[256,2048]{1,0:T(8,128)(2,1)}, u32[]{:S(2)}, u32[]{:S(2)}) collective-permute-start(bf16[256,2048]{1,0:T(8,128)(2,1)} %convolution_convert_fusion.2), channel_id=1, source_target_pairs={{0,1},{1,0},{2,3},{3,2},{4,5},{5,4},{6,7},{7,6},{8,9},{9,8},{10,11... | collective-permute-start | bytes 3145736 | tf_op jit(solution)/shard_map/ppermute | solution.py:295
  196.9 3.0 %copy-start.31 = (bf16[2,1,128,1024]{3,2,1,0:T(8,128)(2,1)S(1)}, bf16[2,1,128,1024]{3,2,1,0:T(8,128)(2,1)}, u32[]{:S(2)}) copy-start(bf16[2,1,128,1024]{3,2,1,0:T(8,128)(2,1)} %get-tuple-element.53) | copy-start | bytes 1572868
  199.1 6.2 %collective-permute-start.8 = (bf16[256,2048]{1,0:T(8,128)(2,1)}, bf16[256,2048]{1,0:T(8,128)(2,1)}, u32[]{:S(2)}, u32[]{:S(2)}) collective-permute-start(bf16[256,2048]{1,0:T(8,128)(2,1)} %convolution_convert_fusion), channel_id=1, source_target_pairs={{0,1},{1,0},{2,3},{3,2},{4,5},{5,4},{6,7},{7,6},{8,9},{9,8},{10,11... | collective-permute-start | bytes 3145736 | tf_op jit(solution)/shard_map/ppermute | solution.py:295
  199.9 5.4 %copy-start.30 = (bf16[2,1,128,1024]{3,2,1,0:T(8,128)(2,1)S(1)}, bf16[2,1,128,1024]{3,2,1,0:T(8,128)(2,1)}, u32[]{:S(2)}) copy-start(bf16[2,1,128,1024]{3,2,1,0:T(8,128)(2,1)} %get-tuple-element.34) | copy-start | bytes 1572868
  199.9 5.4 %copy-start.39 = (bf16[1024,2048]{1,0:T(8,128)(2,1)S(1)}, bf16[1024,2048]{1,0:T(8,128)(2,1)}, u32[]{:S(2)}) copy-start(bf16[1024,2048]{1,0:T(8,128)(2,1)} %param.33) | copy-start | bytes 12582916
  203.8 4.1 %copy-start.27 = (f32[256,2048]{1,0:T(8,128)}, f32[256,2048]{1,0:T(8,128)S(1)}, u32[]{:S(2)}) copy-start(f32[256,2048]{1,0:T(8,128)S(1)} %convert_add_fusion.1) | copy-start | bytes 6291460
  204.8 15.0 %collective-permute-start.4 = (bf16[128,2048]{1,0:T(8,128)(2,1)}, bf16[128,2048]{1,0:T(8,128)(2,1)S(1)}, u32[]{:S(2)}, u32[]{:S(2)}) collective-permute-start(bf16[128,2048]{1,0:T(8,128)(2,1)} %fusion.6), channel_id=1, source_target_pairs={{0,2},{1,3},{2,0},{3,1},{4,6},{5,7},{6,4},{7,5},{8,10},{9,11},{10,... | collective-permute-start | bytes 1572872 | tf_op jit(solution)/shard_map/ppermute | solution.py:302
  207.9 1.4 copy-start.28
  210.1 20.1 %collective-permute-start.9 = (bf16[128,2048]{1,0:T(8,128)(2,1)}, bf16[128,2048]{1,0:T(8,128)(2,1)S(1)}, u32[]{:S(2)}, u32[]{:S(2)}) collective-permute-start(bf16[128,2048]{1,0:T(8,128)(2,1)} %fusion.7), channel_id=1, source_target_pairs={{0,2},{1,3},{2,0},{3,1},{4,6},{5,7},{6,4},{7,5},{8,10},{9,11},{10,... | collective-permute-start | bytes 1572872 | tf_op jit(solution)/shard_map/ppermute | solution.py:302
  211.6 18.6 %copy-start.29 = (f32[256,2048]{1,0:T(8,128)S(1)}, f32[256,2048]{1,0:T(8,128)}, u32[]{:S(2)}) copy-start(f32[256,2048]{1,0:T(8,128)} %copy-done.28) | copy-start | bytes 6291460
  (12 other events, 12.3 us)
Sparse Core Ops, SparseCore 0:
  9.1 25.2 all-gather.4
  36.0 22.5 all-gather.6

commit v3 on v2

--- a/solution.py
+++ b/solution.py
@@ -217,13 +217,8 @@
     )(query, base, gate, states, gain.reshape(1, dim))
 
 
-def augment(tokens, lengths, headers):
-    tok = tokens.shape[0]
-    place = lax.axis_index("ctx")
-    parts = lax.axis_size("ctx")
-    longest = tok * parts // 16
-    hops = -(-(longest - 1) // tok)
-    position = place * tok + jnp.arange(tok, dtype=jnp.int32)
+def region_masks(lengths, headers, tok):
+    position = lax.axis_index("ctx") * tok + jnp.arange(tok, dtype=jnp.int32)
     ends = jnp.cumsum(lengths)
     starts = ends - lengths
     span = jnp.minimum(headers, lengths)
@@ -233,19 +228,47 @@
     def holds(point):
         return ((starts <= point) & (point < ends))[:, None]
 
-    sums = jnp.einsum("rt,td->rd", header.astype(BF16), tokens, preferred_element_type=F32)
+    return inside, header, span, holds
+
+
+def header_sums(header, tokens):
+    return jnp.einsum("rt,td->rd", header.astype(BF16), tokens, preferred_element_type=F32)
+
+
+def boundary_sums(tokens, masks):
+    seqs, tok, part = tokens.shape
+    place = lax.axis_index("ctx")
+    longest = tok * lax.axis_size("ctx") // 16
+    hops = -(-(longest - 1) // tok)
+    sums = [header_sums(masks[seq][1], tokens[seq]) for seq in range(seqs)]
 
     def part_at(point):
-        return jnp.sum(jnp.where(holds(point), sums, 0.0), axis=0, keepdims=True)
+        return jnp.stack(
+            [
+                jnp.sum(jnp.where(masks[seq][3](point), sums[seq], 0.0), axis=0)
+                for seq in range(seqs)
+            ]
+        )
 
     before = shifted(part_at((place + 1) * tok), "ctx", 1)
     for hop in range(2, hops + 1):
         before = before + shifted(part_at((place + hop) * tok), "ctx", hop)
     after = shifted(part_at(place * tok), "ctx", -1)
+    size = lax.axis_size("head")
+    both = jnp.concatenate([before, after])
+    spread = jnp.broadcast_to(both, (size,) + both.shape)
+    held = lax.all_to_all(spread, "head", 0, 0, tiled=True)
+    return held.transpose(1, 0, 2).reshape(2, seqs, size * part)
+
+
+def augment(tokens, masks, before, after):
+    tok = tokens.shape[0]
+    place = lax.axis_index("ctx")
+    inside, header, span, holds = masks
     totals = (
-        sums
-        + jnp.where(holds(place * tok), before, 0.0)
-        + jnp.where(holds((place + 1) * tok), after, 0.0)
+        header_sums(header, tokens)
+        + jnp.where(holds(place * tok), before[None, :], 0.0)
+        + jnp.where(holds((place + 1) * tok), after[None, :], 0.0)
     )
     means = totals / span[:, None].astype(F32)
     top = means.astype(BF16)
@@ -260,12 +283,14 @@
     return (tokens.astype(F32) + added).astype(BF16)
 
 
-def incoming_states(maps, dim):
+def incoming_states(maps, dim, first):
     heads = maps.shape[0]
     parts = lax.axis_size("ctx")
     if heads % parts == 0:
         sent = maps.reshape(parts, heads // parts, dim, 2 * dim)
         held = lax.all_to_all(sent, "ctx", 0, 0, tiled=True)
+        if first is not None:
+            held, _ = lax.optimization_barrier((held, first))
         states = lax.all_to_all(prefix_states(held), "ctx", 0, 0, tiled=True)
         return states.reshape(heads, dim, dim)
 
@@ -275,14 +300,15 @@
         ) + maps[..., dim:].astype(F32)
         return shifted(moved.astype(BF16), "ctx", 1)
 
-    return lax.fori_loop(0, parts - 1, relay, jnp.zeros((heads, dim, dim), BF16))
-
-
-def head_sum(hidden, w_out):
+    states = lax.fori_loop(0, parts - 1, relay, jnp.zeros((heads, dim, dim), BF16))
+    return states
+
+
+def core_sum(hidden, w_out):
     size = lax.axis_size("head")
     me = lax.axis_index("head")
     chips = size // 2
-    core, chip = me % 2, me // 2
+    core = me % 2
     rows = hidden.shape[0] // size
     cut = hidden.reshape(chips, 2, rows, hidden.shape[1])
 
@@ -294,7 +320,13 @@
 
     arrived = lax.ppermute(half(1 - core), "head", [(i, i ^ 1) for i in range(size)])
     both = half(core).astype(F32) + arrived.astype(F32)
-    both = both.reshape(chips, rows, w_out.shape[1])
+    return both.reshape(chips, rows, w_out.shape[1])
+
+
+def chip_sum(both):
+    size = lax.axis_size("head")
+    chips = size // 2
+    chip = lax.axis_index("head") // 2
     total = lax.dynamic_index_in_dim(both, chip, 0, keepdims=False)
     for step in range(1, chips):
         leaving = lax.dynamic_index_in_dim(both, (chip + step) % chips, 0, keepdims=False)
@@ -333,11 +365,14 @@
     places = jnp.arange(CHUNK)
     below = (places[:, None] >= places[None, :]).astype(F32)
 
+    masks = [region_masks(region_lengths[i], header_lengths[i], tok) for i in range(seqs)]
+    carried = boundary_sums(tokens, masks)
+
     def one(seq, earlier):
         raw = lax.all_gather(tokens[seq], "head", axis=1, tiled=True)
         if earlier is not None:
-            raw, _ = lax.optimization_barrier((raw, earlier))
-        whole = augment(raw, region_lengths[seq], header_lengths[seq])
+            raw, _ = lax.optimization_barrier((raw, earlier[0]))
+        whole = augment(raw, masks[seq], carried[0, seq], carried[1, seq])
 
         def project(weight):
             return jnp.dot(whole, weight, preferred_element_type=F32)
@@ -356,12 +391,18 @@
         rows = cumul.transpose(1, 2, 0)
         rim = jnp.pad(rim.astype(F32), ((5, 0), (0, 0)))
         rims = (rim[:, :width], rim[:, width : 2 * width], rim[:, 2 * width :])
+        if earlier is not None:
+            rows, _ = lax.optimization_barrier((rows, earlier[1]))
         maps, query_total, base_total = delta_local(
             *raws, rims, (conv_query, conv_key, conv_value), cols, rows, dim
         )
-        states = incoming_states(maps, dim)
+        states = incoming_states(maps, dim, None if earlier is None else earlier[2])
+        if earlier is not None:
+            states, _ = lax.optimization_barrier((states, earlier[3]))
         hidden = finish(query_total, base_total, gate_raw, states, norm_gain)
-        return head_sum(hidden, w_out), maps
+        both = core_sum(hidden, w_out)
+        mixed = chip_sum(both)
+        return mixed, (maps, states, both, mixed)
 
     mixed, earlier = [], None
     for seq in range(seqs):

time: 240 us -> 217 us (0.904)
  starting transfers between devices: 43.3 us -> 34.6 us
  matrix products: 47.1 us -> 40.5 us
  local copies, waits for them, and re-layouts: 27.5 us -> 23 us
  waiting for transfers between devices: 56.2 us -> 53.1 us
    all_gather x2, waiting for transfers between devices: 23.8 us -> 8.05 us  [one(): raw = lax.all_gather(tokens[seq], 'head', axis=1, tiled=True)]
    all_to_all x2, waiting for transfers between devices: 0.35 us -> 9.68 us  [incoming_states(): states = lax.all_to_all(prefix_states(held), 'ctx', 0, 0, tiled=True)]
    all_to_all x2, starting transfers between devices: 12.9 us -> 8.42 us  [incoming_states(): held = lax.all_to_all(sent, 'ctx', 0, 0, tiled=True)]
    all_to_all x2, waiting for transfers between devices: 8.55 us -> 12.8 us  [incoming_states(): held = lax.all_to_all(sent, 'ctx', 0, 0, tiled=True)]
    all_to_all x0 -> x1, waiting for transfers between devices: none -> 4.16 us  [boundary_sums(): held = lax.all_to_all(spread, 'head', 0, 0, tiled=True)]
    ppermute x6 -> x4, starting transfers between devices: 18.4 us -> 14.4 us  [shifted(): return lax.ppermute(shard, axis, pairs)]
    dot_general x10, matrix products: 28.2 us -> 24.6 us  [project(): return jnp.dot(whole, weight, preferred_element_type=F32)]
    unnamed x89 -> x93, local copies, waits for them, and re-layouts: 18.7 us -> 15.3 us
  transfers between devices with their start and end apart: 16 -> 15, of which waited for: 8 -> 10; matrix products, arithmetic and copies ran while one was open for 21% -> 18% of each run, Pallas kernels for 18% -> 18%
where the time goes in v3:
time: 217 us; the launch traced here: 216 us
  waiting for transfers between devices  53.1 us (24%)
  Pallas kernels  45.2 us (21%)
  matrix products  40.5 us (19%)
  starting transfers between devices  34.6 us (16%)
  local copies, waits for them, and re-layouts  23 us (11%)
  between operations  14.2 us (7%)
  other arithmetic  5.04 us (2%)
    pallas_call x2, Pallas kernels, delta_local(): pl.pallas_call(delta_kernel, grid=(groups,), in_specs=[narrow, narrow, br...  37.2 us
    dot_general x10, matrix products, project(): return jnp.dot(whole, weight, preferred_element_type=F32)  24.6 us
    unnamed x93, local copies, waits for them, and re-layouts  15.3 us
    ppermute x4, starting transfers between devices, shifted(): return lax.ppermute(shard, axis, pairs)  14.4 us
    ppermute x2, waiting for transfers between devices, chip_sum(): lax.ppermute(leaving.astype(BF16), 'head', pairs).astype(F32)  13.5 us
    all_to_all x2, waiting for transfers between devices, incoming_states(): held = lax.all_to_all(sent, 'ctx', 0, 0, tiled=True)  12.8 us
    all_to_all x2, waiting for transfers between devices, incoming_states(): states = lax.all_to_all(prefix_states(held), 'ctx', 0, 0, tiled=True)  9.68 us
    dot_general x4, matrix products, half(): jnp.dot(picked.reshape(chips * rows, hidden.shape[1]), w_out, preferred_e...  8.85 us
  transfers between devices with their start and end apart: 15, of which 10 were waited for; matrix products, arithmetic and copies ran while one was open for 18% of the time, Pallas kernels for 18%

profile of v3, /device:TPU:0, one launch (start us, length us, event | category | flops | bytes accessed | tf_op | source)
XLA Modules:
  0.0 215.6 jit_solution(9333528543658814463)
XLA Ops:
  6.6 2.4 %fusion.83 = (bf16[1,512,512]{2,1,0:T(8,128)(2,1)}, bf16[1,512,512]{2,1,0:T(8,128)(2,1)}) fusion(bf16[2,512,512]{2,1,0:T(8,128)(2,1)} %param.17), kind=kLoop, calls=%fused_computation.151 | loop fusion | bytes 2097152 | tf_op jit(solution)/shard_map/slice | solution.py:372
  10.3 1.3 collective-permute-start.1
  11.7 5.5 %collective-permute-start = (f32[2,512]{1,0:T(2,128)S(1)}, f32[2,512]{1,0:T(2,128)S(1)}, u32[]{:S(2)}, u32[]{:S(2)}) collective-permute-start(f32[2,512]{1,0:T(2,128)S(1)} %pad_maximum_fusion.4), channel_id=1, source_target_pairs={{0,4},{4,8},{8,12},{12,16},{16,20},{20,24},{24,28},{1,5},{5,9},{9,... | collective-permute-start | bytes 12296 | tf_op jit(solution)/shard_map/ppermute | solution.py:17
  17.3 1.1 collective-permute-done
  19.1 3.3 %all-to-all-start = ((f32[4,4,512]{2,1,0:T(4,128)}), f32[4,4,512]{2,1,0:T(4,128)S(1)}, u32[]{:S(2)}, u32[]{:S(2)}) async-start(f32[4,4,512]{2,1,0:T(4,128)} %broadcast_in_dim.130), calls=%async_computation | async-start | bytes 65536 | tf_op jit(solution)/shard_map/all_to_all | solution.py:260
  22.5 4.2 %all-to-all-done = f32[4,4,512]{2,1,0:T(4,128)S(1)} async-done(((f32[4,4,512]{2,1,0:T(4,128)}), f32[4,4,512]{2,1,0:T(4,128)S(1)}, u32[]{:S(2)}, u32[]{:S(2)}) %all-to-all-start) | async-done | bytes 32800 | tf_op jit(solution)/shard_map/all_to_all | solution.py:260
  26.8 8.1 %all-gather.5.cloned.1.call-done = bf16[1,512,2048]{2,1,0:T(8,128)(2,1)} async-done(((bf16[1,512,512]{2,1,0:T(8,128)(2,1)}), bf16[1,512,2048]{2,1,0:T(8,128)(2,1)}) %all-gather.5.cloned.1.call-update) | async-done | bytes 2097168 | tf_op jit(solution)/shard_map/all_gather | solution.py:372
  34.8 2.3 %subtract_convert_fusion.1 = (bf16[64,2048]{1,0:T(8,128)(2,1)S(1)}, bf16[64,2048]{1,0:T(8,128)(2,1)S(1)}) fusion(f32[64]{0:T(128)S(1)} %get-tuple-element.54, f32[2048]{0:T(1024)S(1)} %bitcast.168, pred[64]{0:T(512)(128)(4,1)S(1)} %compare_and_fusion.10, f32[2048]{0:T(1024)S(1)} %bitcast.169, pred[64]{0:T(512)(128)(4,1)S(1)} %get-tuple-element.33, ...), kind=kOutput, calls=%fused_computation.48 | convolution fusion | flops 135561216 | bytes 2641024 | tf_op jit(solution)/shard_map/rt,td->rd/dot_general | solution.py:235
  38.5 2.1 convolution_convert_fusion.10.k_ref
  40.6 2.1 convolution_convert_fusion.11.q_ref
  43.1 2.4 %convolution_convert_fusion.7.v_ref = bf16[512,1024]{1,0:T(8,128)(2,1)S(1)} fusion(bf16[512,2048]{1,0:T(8,128)(2,1)S(1)} %add_convert_fusion.1, bf16[2048,1024]{1,0:T(8,128)(2,1)S(1)} %copy-done.38), kind=kOutput, calls=%fused_computation.20 | convolution fusion | flops 2148007936 | bytes 7340032 | tf_op jit(solution)/shard_map/dot_general | solution.py:378
  47.4 3.5 %collective-permute-start.2 = (bf16[3,2048]{1,0:T(4,128)(2,1)S(1)}, bf16[3,2048]{1,0:T(4,128)(2,1)S(1)}, u32[]{:S(2)}, u32[]{:S(2)}) collective-permute-start(bf16[3,2048]{1,0:T(4,128)(2,1)S(1)} %pad_maximum_fusion.1), channel_id=1, source_target_pairs={{0,4},{4,8},{8,12},{12,16},{16,20},{20,24},{24,28},{1,5},{5,9},{9,... | collective-permute-start | bytes 36872 | tf_op jit(solution)/shard_map/ppermute | solution.py:17
  50.9 6.2 %convolution_convert_fusion.6.gate_ref = bf16[512,1024]{1,0:T(8,128)(2,1)} fusion(bf16[512,2048]{1,0:T(8,128)(2,1)} %copy-done.27, bf16[2048,1024]{1,0:T(8,128)(2,1)} %param.23), kind=kOutput, calls=%fused_computation.19 | convolution fusion | flops 2148007936 | bytes 7340032 | tf_op jit(solution)/shard_map/dot_general | solution.py:378
  57.5 1.2 copy-done.5
  58.8 1.0 copy-done.10
  60.8 18.6 %shard_map.163 = (bf16[8,128,256]{2,1,0:T(8,128)(2,1)}, bf16[512,1024]{1,0:T(8,128)(2,1)S(1)}, f32[512,1024]{1,0:T(8,128)}) custom-call(bf16[512,512]{1,0:T(8,128)(2,1)S(1)} %copy-done.11, bf16[512,512]{1,0:T(8,128)(2,1)S(1)} %copy-done.10, bf16[512,1024]{1,0:T(8,128)(2,1)S(1)} %copy-done.5, f32[8,512]{1,0:T(8,128)S(1)} %get-tuple-element.50.rq_ref, ...), custom_call_target="tpu_custom_call" | custom-call | flops 20132659200 | bytes 8388608 | tf_op jit(solution)/shard_map/pallas_call | solution.py:131
  80.4 2.3 %subtract_convert_fusion = (bf16[64,2048]{1,0:T(8,128)(2,1)S(1)}, bf16[64,2048]{1,0:T(8,128)(2,1)S(1)}) fusion(f32[64]{0:T(128)S(1)} %get-tuple-element.53, f32[2048]{0:T(1024)S(1)} %bitcast.167, pred[64]{0:T(512)(128)(4,1)S(1)} %compare_and_fusion.9, f32[2048]{0:T(1024)S(1)} %bitcast.166, pred[64]{0:T(512)(128)(4,1)S(1)} %get-tuple-element.57, ...), kind=kOutput, calls=%fused_computation.47 | convolution fusion | flops 135561216 | bytes 2641024 | tf_op jit(solution)/shard_map/rt,td->rd/dot_general | solution.py:235
  84.5 1.2 convolution_convert_fusion.8.k_ref
  85.8 4.7 %all-to-all-start.1 = ((bf16[8,1,128,256]{3,2,1,0:T(8,128)(2,1)}), bf16[8,1,128,256]{3,2,1,0:T(8,128)(2,1)S(1)}, u32[]{:S(2)}, u32[]{:S(2)}) async-start(bf16[8,1,128,256]{3,2,1,0:T(8,128)(2,1)} %bitcast.21), calls=%async_computation.1 | async-start | bytes 1048576 | tf_op jit(solution)/shard_map/all_to_all | solution.py:291
  90.5 3.6 %convolution_convert_fusion.9.q_ref = bf16[512,512]{1,0:T(8,128)(2,1)S(1)} fusion(bf16[512,2048]{1,0:T(8,128)(2,1)} %copy-done.24, bf16[2048,512]{1,0:T(8,128)(2,1)} %param.20), kind=kOutput, calls=%fused_computation.22 | convolution fusion | flops 1074003968 | bytes 4718592 | tf_op jit(solution)/shard_map/dot_general | solution.py:378
  95.0 2.4 %convolution_convert_fusion.5.v_ref = bf16[512,1024]{1,0:T(8,128)(2,1)S(1)} fusion(bf16[512,2048]{1,0:T(8,128)(2,1)S(1)} %copy-done.25, bf16[2048,1024]{1,0:T(8,128)(2,1)S(1)} %copy-done.39), kind=kOutput, calls=%fused_computation.18 | convolution fusion | flops 2148007936 | bytes 7340032 | tf_op jit(solution)/shard_map/dot_general | solution.py:378
  98.3 6.7 %all-to-all-done.1.maps_ref = bf16[8,1,128,256]{3,2,1,0:T(8,128)(2,1)S(1)} async-done(((bf16[8,1,128,256]{3,2,1,0:T(8,128)(2,1)}), bf16[8,1,128,256]{3,2,1,0:T(8,128)(2,1)S(1)}, u32[]{:S(2)}, u32[]{:S(2)}) %all-to-all-start.1) | async-done | bytes 524320 | tf_op jit(solution)/shard_map/all_to_all | solution.py:291
  105.1 1.8 shard_map.164
  106.8 3.6 %all-to-all-start.2 = ((bf16[8,1,128,128]{3,2,1,0:T(8,128)(2,1)}), bf16[8,1,128,128]{3,2,1,0:T(8,128)(2,1)S(1)}, u32[]{:S(2)}, u32[]{:S(2)}) async-start(bf16[8,1,128,128]{3,2,1,0:T(8,128)(2,1)} %shard_map.164), calls=%async_computation.2 | async-start | bytes 524288 | tf_op jit(solution)/shard_map/all_to_all | solution.py:294
  111.1 4.1 %collective-permute-start.5 = (bf16[3,2048]{1,0:T(4,128)(2,1)}, bf16[3,2048]{1,0:T(4,128)(2,1)S(1)}, u32[]{:S(2)}, u32[]{:S(2)}) collective-permute-start(bf16[3,2048]{1,0:T(4,128)(2,1)} %pad_maximum_fusion.2), channel_id=1, source_target_pairs={{0,4},{4,8},{8,12},{12,16},{16,20},{20,24},{24,28},{1,5},{5,9},{9,... | collective-permute-start | bytes 36872 | tf_op jit(solution)/shard_map/ppermute | solution.py:17
  116.6 2.9 %all-to-all-done.2 = bf16[8,1,128,128]{3,2,1,0:T(8,128)(2,1)S(1)} async-done(((bf16[8,1,128,128]{3,2,1,0:T(8,128)(2,1)}), bf16[8,1,128,128]{3,2,1,0:T(8,128)(2,1)S(1)}, u32[]{:S(2)}, u32[]{:S(2)}) %all-to-all-start.2) | async-done | bytes 262176 | tf_op jit(solution)/shard_map/all_to_all | solution.py:294
  119.6 1.6 copy-done.16
  121.2 1.2 copy-done.18
  122.4 1.2 copy-done.20
  123.6 2.2 %shard_map.165 = bf16[512,1024]{1,0:T(8,128)(2,1)S(1)} custom-call(bf16[512,1024]{1,0:T(8,128)(2,1)S(1)} %copy-done.20, f32[512,1024]{1,0:T(8,128)S(1)} %copy-done.16, bf16[512,1024]{1,0:T(8,128)(2,1)S(1)} %copy-done.18, bf16[8,128,128]{2,1,0:T(8,128)(2,1)S(1)} %bitcast.148, f32[1,128]{1,0:T(1,128)S(1)} %bitcast.152), custom_call_target="tpu_custom_call" | custom-call | flops 2147483648 | bytes 8388608 | tf_op jit(solution)/shard_map/pallas_call | solution.py:203
  126.8 2.2 %convolution_convert_fusion.2 = bf16[256,2048]{1,0:T(8,128)(2,1)} fusion(bf16[256,1024]{1,0:T(8,128)(2,1)S(1)} %bitcast.164, bf16[1024,2048]{1,0:T(8,128)(2,1)S(1)} %copy-done.41), kind=kOutput, calls=%fused_computation.5 | convolution fusion | flops 1074266112 | bytes 5767168 | tf_op jit(solution)/shard_map/dot_general | solution.py:317
  129.1 18.6 %shard_map.166 = (bf16[8,128,256]{2,1,0:T(8,128)(2,1)S(1)}, bf16[512,1024]{1,0:T(8,128)(2,1)S(1)}, f32[512,1024]{1,0:T(8,128)}) custom-call(bf16[512,512]{1,0:T(8,128)(2,1)S(1)} %copy-done.9, bf16[512,512]{1,0:T(8,128)(2,1)S(1)} %copy-done.7, bf16[512,1024]{1,0:T(8,128)(2,1)S(1)} %copy-done.3, f32[8,512]{1,0:T(8,128)S(1)} %get-tuple-element.48.rq_ref, ...), custom_call_target="tpu_custom_call" | custom-call | flops 20132659200 | bytes 8388608 | tf_op jit(solution)/shard_map/pallas_call | solution.py:131
  149.4 3.8 %all-to-all-start.3 = ((bf16[8,1,128,256]{3,2,1,0:T(8,128)(2,1)}), bf16[8,1,128,256]{3,2,1,0:T(8,128)(2,1)S(1)}, u32[]{:S(2)}, u32[]{:S(2)}) async-start(bf16[8,1,128,256]{3,2,1,0:T(8,128)(2,1)} %bitcast.147), calls=%async_computation.3 | async-start | bytes 1048576 | tf_op jit(solution)/shard_map/all_to_all | solution.py:291
  153.2 4.1 %convert_add_fusion.1 = f32[256,2048]{1,0:T(8,128)S(1)} fusion(bf16[256,2048]{1,0:T(8,128)(2,1)} %collective-permute-done.3, bf16[256,1024]{1,0:T(8,128)(2,1)} %bitcast.161, bf16[1024,2048]{1,0:T(8,128)(2,1)} %param.33), kind=kOutput, calls=%fused_computation.16 | convolution fusion | flops 1075838976 | bytes 7864320 | tf_op jit(solution)/shard_map/dot_general | solution.py:317
  158.8 3.4 %convolution_convert_fusion.4.gate_ref = bf16[512,1024]{1,0:T(8,128)(2,1)} fusion(bf16[512,2048]{1,0:T(8,128)(2,1)S(1)} %copy-done.26, bf16[2048,1024]{1,0:T(8,128)(2,1)S(1)} %copy-done.40), kind=kOutput, calls=%fused_computation.17 | convolution fusion | flops 2148007936 | bytes 7340032 | tf_op jit(solution)/shard_map/dot_general | solution.py:378
  162.2 6.1 %all-to-all-done.3.maps_ref = bf16[8,1,128,256]{3,2,1,0:T(8,128)(2,1)S(1)} async-done(((bf16[8,1,128,256]{3,2,1,0:T(8,128)(2,1)}), bf16[8,1,128,256]{3,2,1,0:T(8,128)(2,1)S(1)}, u32[]{:S(2)}, u32[]{:S(2)}) %all-to-all-start.3) | async-done | bytes 524320 | tf_op jit(solution)/shard_map/all_to_all | solution.py:291
  168.3 1.8 shard_map.167
  170.1 3.8 %all-to-all-start.4 = ((bf16[8,1,128,128]{3,2,1,0:T(8,128)(2,1)}), bf16[8,1,128,128]{3,2,1,0:T(8,128)(2,1)S(1)}, u32[]{:S(2)}, u32[]{:S(2)}) async-start(bf16[8,1,128,128]{3,2,1,0:T(8,128)(2,1)} %shard_map.167), calls=%async_computation.4 | async-start | bytes 524288 | tf_op jit(solution)/shard_map/all_to_all | solution.py:294
  173.9 2.3 %fusion.8 = bf16[128,2048]{1,0:T(8,128)(2,1)} fusion(bf16[128,2048]{1,0:T(8,128)(2,1)} %collective-permute-done.4, f32[2,128,2048]{2,1,0:T(8,128)} %bitcast.158, s32[]{:T(128)S(6)} %select_n.82), kind=kLoop, calls=%fused_computation.31 | loop fusion | flops 786432 | bytes 2097156 | tf_op jit(solution)/shard_map/convert_element_type | solution.py:335
  176.2 6.8 %all-to-all-done.4 = bf16[8,1,128,128]{3,2,1,0:T(8,128)(2,1)S(1)} async-done(((bf16[8,1,128,128]{3,2,1,0:T(8,128)(2,1)}), bf16[8,1,128,128]{3,2,1,0:T(8,128)(2,1)S(1)}, u32[]{:S(2)}, u32[]{:S(2)}) %all-to-all-start.4) | async-done | bytes 262176 | tf_op jit(solution)/shard_map/all_to_all | solution.py:294
  183.0 1.6 copy-done.17
  184.6 1.2 copy-done.23
  185.8 2.2 %shard_map.168 = bf16[512,1024]{1,0:T(8,128)(2,1)S(1)} custom-call(bf16[512,1024]{1,0:T(8,128)(2,1)S(1)} %copy-done.22, f32[512,1024]{1,0:T(8,128)S(1)} %copy-done.17, bf16[512,1024]{1,0:T(8,128)(2,1)S(1)} %copy-done.23, bf16[8,128,128]{2,1,0:T(8,128)(2,1)S(1)} %bitcast.149, f32[1,128]{1,0:T(1,128)S(1)} %bitcast.153), custom_call_target="tpu_custom_call" | custom-call | flops 2147483648 | bytes 8388608 | tf_op jit(solution)/shard_map/pallas_call | solution.py:203
  188.2 1.3 convolution_convert_fusion
  189.5 2.6 %collective-permute-done.6 = bf16[256,2048]{1,0:T(8,128)(2,1)S(1)} collective-permute-done((bf16[256,2048]{1,0:T(8,128)(2,1)S(1)}, bf16[256,2048]{1,0:T(8,128)(2,1)S(1)}, u32[]{:S(2)}, u32[]{:S(2)}) %collective-permute-start.6) | collective-permute-done | bytes 1048608 | tf_op jit(solution)/shard_map/ppermute | solution.py:321
  192.2 1.3 convert_add_fusion
  194.1 13.5 %collective-permute-done.7 = bf16[128,2048]{1,0:T(8,128)(2,1)S(1)} collective-permute-done((bf16[128,2048]{1,0:T(8,128)(2,1)S(1)}, bf16[128,2048]{1,0:T(8,128)(2,1)S(1)}, u32[]{:S(2)}, u32[]{:S(2)}) %collective-permute-start.7) | collective-permute-done | bytes 524320 | tf_op jit(solution)/shard_map/ppermute | solution.py:334
  207.7 1.1 pad_maximum_fusion
  (159 shorter events, 19.0 us)
Async XLA Ops:
  6.5 32.0 %copy-start = (bf16[2048,512]{1,0:T(8,128)(2,1)S(1)}, bf16[2048,512]{1,0:T(8,128)(2,1)}, u32[]{:S(2)}) copy-start(bf16[2048,512]{1,0:T(8,128)(2,1)} %param.21) | copy-start | bytes 6291460
  6.5 3.2 %copy-start.32 = (bf16[2,512,512]{2,1,0:T(8,128)(2,1)S(1)}, bf16[2,512,512]{2,1,0:T(8,128)(2,1)}, u32[]{:S(2)}) copy-start(bf16[2,512,512]{2,1,0:T(8,128)(2,1)} %param.17) | copy-start | bytes 3145732
  6.5 2.5 %copy-start.35 = (s32[2,64]{1,0:T(2,128)S(1)}, s32[2,64]{1,0:T(2,128)}, u32[]{:S(2)}) copy-start(s32[2,64]{1,0:T(2,128)} %param.18) | copy-start | bytes 1540
  6.5 3.2 %copy-start.37 = (s32[2,64]{1,0:T(2,128)S(1)}, s32[2,64]{1,0:T(2,128)}, u32[]{:S(2)}) copy-start(s32[2,64]{1,0:T(2,128)} %param.19) | copy-start | bytes 1540
  6.5 28.3 %all-gather.5.cloned.1.call-start = ((), (), s32[]{:S(2)}) async-start(), calls=%async_computation.5 | async-start | bytes 2621440 | tf_op jit(solution)/shard_map/all_gather | solution.py:372
  9.0 8.3 %copy-start.33 = (bf16[2048,8]{0,1:T(8,128)(2,1)S(1)}, bf16[2048,8]{0,1:T(8,128)(2,1)}, u32[]{:S(2)}) copy-start(bf16[2048,8]{0,1:T(8,128)(2,1)} %param.24) | copy-start | bytes 98308
  9.0 13.4 %copy-start.34 = (bf16[2048,8]{0,1:T(8,128)(2,1)S(1)}, bf16[2048,8]{0,1:T(8,128)(2,1)}, u32[]{:S(2)}) copy-start(bf16[2048,8]{0,1:T(8,128)(2,1)} %param.25) | copy-start | bytes 98308
  9.0 13.5 %copy-start.44 = (f32[8]{0:T(128)S(1)}, f32[8]{0:T(128)}, u32[]{:S(2)}) copy-start(f32[8]{0:T(128)} %param.29) | copy-start | bytes 100
  9.0 71.4 %all-gather.7.cloned.1.call-start = ((), (), s32[]{:S(2)}) async-start(), calls=%async_computation.6 | async-start | bytes 2621440 | tf_op jit(solution)/shard_map/all_gather | solution.py:372
  10.3 7.0 %collective-permute-start.1 = (f32[2,512]{1,0:T(2,128)S(1)}, f32[2,512]{1,0:T(2,128)S(1)}, u32[]{:S(2)}, u32[]{:S(2)}) collective-permute-start(f32[2,512]{1,0:T(2,128)S(1)} %pad_maximum_fusion.5), channel_id=1, source_target_pairs={{4,0},{8,4},{12,8},{16,12},{20,16},{24,20},{28,24},{5,1},{9,5},{13... | collective-permute-start | bytes 12296 | tf_op jit(solution)/shard_map/ppermute | solution.py:17
  11.7 6.8 %collective-permute-start = (f32[2,512]{1,0:T(2,128)S(1)}, f32[2,512]{1,0:T(2,128)S(1)}, u32[]{:S(2)}, u32[]{:S(2)}) collective-permute-start(f32[2,512]{1,0:T(2,128)S(1)} %pad_maximum_fusion.4), channel_id=1, source_target_pairs={{0,4},{4,8},{8,12},{12,16},{16,20},{20,24},{24,28},{1,5},{5,9},{9,... | collective-permute-start | bytes 12296 | tf_op jit(solution)/shard_map/ppermute | solution.py:17
  19.1 7.6 %all-to-all-start = ((f32[4,4,512]{2,1,0:T(4,128)}), f32[4,4,512]{2,1,0:T(4,128)S(1)}, u32[]{:S(2)}, u32[]{:S(2)}) async-start(f32[4,4,512]{2,1,0:T(4,128)} %broadcast_in_dim.130), calls=%async_computation | async-start | bytes 65536 | tf_op jit(solution)/shard_map/all_to_all | solution.py:260
  34.8 2.3 %copy-start.28 = (bf16[1,512,2048]{2,1,0:T(8,128)(2,1)S(1)}, bf16[1,512,2048]{2,1,0:T(8,128)(2,1)}, u32[]{:S(2)}) copy-start(bf16[1,512,2048]{2,1,0:T(8,128)(2,1)} %all-gather.5.cloned.1.call-done) | copy-start | bytes 6291460
  37.9 4.8 %copy-start.27 = (bf16[512,2048]{1,0:T(8,128)(2,1)}, bf16[512,2048]{1,0:T(8,128)(2,1)S(1)}, u32[]{:S(2)}) copy-start(bf16[512,2048]{1,0:T(8,128)(2,1)S(1)} %add_convert_fusion.1) | copy-start | bytes 6291460
  38.5 2.1 copy-start.43
  40.6 2.5 %copy-start.38 = (bf16[2048,1024]{1,0:T(8,128)(2,1)S(1)}, bf16[2048,1024]{1,0:T(8,128)(2,1)}, u32[]{:S(2)}) copy-start(bf16[2048,1024]{1,0:T(8,128)(2,1)} %param.22) | copy-start | bytes 12582916
  43.1 2.4 %copy-start.45 = (f32[8]{0:T(128)S(1)}, f32[8]{0:T(128)}, u32[]{:S(2)}) copy-start(f32[8]{0:T(128)} %param.30) | copy-start | bytes 100
  43.1 2.6 %copy-start.36 = (f32[8]{0:T(128)S(1)}, f32[8]{0:T(128)}, u32[]{:S(2)}) copy-start(f32[8]{0:T(128)} %param.31) | copy-start | bytes 100
  45.5 11.6 %copy-start.4 = (bf16[512,1024]{1,0:T(8,128)(2,1)}, bf16[512,1024]{1,0:T(8,128)(2,1)S(1)}, u32[]{:S(2)}) copy-start(bf16[512,1024]{1,0:T(8,128)(2,1)S(1)} %convolution_convert_fusion.7.v_ref) | copy-start | bytes 3145732
  47.3 10.2 %copy-start.12 = (f32[4,1024]{1,0:T(4,128)S(1)}, f32[4,1024]{1,0:T(4,128)}, u32[]{:S(2)}) copy-start(f32[4,1024]{1,0:T(4,128)} %tv_ref.3) | copy-start | bytes 49156
  47.4 10.2 %copy-start.13 = (f32[4,512]{1,0:T(4,128)S(1)}, f32[4,512]{1,0:T(4,128)}, u32[]{:S(2)}) copy-start(f32[4,512]{1,0:T(4,128)} %tq_ref.3) | copy-start | bytes 24580
  47.4 10.2 %copy-start.14 = (f32[4,512]{1,0:T(4,128)S(1)}, f32[4,512]{1,0:T(4,128)}, u32[]{:S(2)}) copy-start(f32[4,512]{1,0:T(4,128)} %tk_ref.3) | copy-start | bytes 24580
  47.4 10.1 %collective-permute-start.2 = (bf16[3,2048]{1,0:T(4,128)(2,1)S(1)}, bf16[3,2048]{1,0:T(4,128)(2,1)S(1)}, u32[]{:S(2)}, u32[]{:S(2)}) collective-permute-start(bf16[3,2048]{1,0:T(4,128)(2,1)S(1)} %pad_maximum_fusion.1), channel_id=1, source_target_pairs={{0,4},{4,8},{8,12},{12,16},{16,20},{20,24},{24,28},{1,5},{5,9},{9,... | collective-permute-start | bytes 36872 | tf_op jit(solution)/shard_map/ppermute | solution.py:17
  80.4 2.3 %copy-start.29 = (bf16[1,512,2048]{2,1,0:T(8,128)(2,1)S(1)}, bf16[1,512,2048]{2,1,0:T(8,128)(2,1)}, u32[]{:S(2)}) copy-start(bf16[1,512,2048]{2,1,0:T(8,128)(2,1)} %all-gather.7.cloned.1.call-done) | copy-start | bytes 6291460
  83.5 2.3 %copy-start.24 = (bf16[512,2048]{1,0:T(8,128)(2,1)}, bf16[512,2048]{1,0:T(8,128)(2,1)S(1)}, u32[]{:S(2)}) copy-start(bf16[512,2048]{1,0:T(8,128)(2,1)S(1)} %add_convert_fusion) | copy-start | bytes 6291460
  85.8 8.4 %copy-start.6 = (bf16[512,512]{1,0:T(8,128)(2,1)}, bf16[512,512]{1,0:T(8,128)(2,1)S(1)}, u32[]{:S(2)}) copy-start(bf16[512,512]{1,0:T(8,128)(2,1)S(1)} %convolution_convert_fusion.8.k_ref) | copy-start | bytes 1572868
  85.8 19.3 %all-to-all-start.1 = ((bf16[8,1,128,256]{3,2,1,0:T(8,128)(2,1)}), bf16[8,1,128,256]{3,2,1,0:T(8,128)(2,1)S(1)}, u32[]{:S(2)}, u32[]{:S(2)}) async-start(bf16[8,1,128,256]{3,2,1,0:T(8,128)(2,1)} %bitcast.21), calls=%async_computation.1 | async-start | bytes 1048576 | tf_op jit(solution)/shard_map/all_to_all | solution.py:291
  90.5 4.5 %copy-start.25 = (bf16[512,2048]{1,0:T(8,128)(2,1)S(1)}, bf16[512,2048]{1,0:T(8,128)(2,1)}, u32[]{:S(2)}) copy-start(bf16[512,2048]{1,0:T(8,128)(2,1)} %copy-done.24) | copy-start | bytes 6291460
  90.5 4.5 %copy-start.39 = (bf16[2048,1024]{1,0:T(8,128)(2,1)S(1)}, bf16[2048,1024]{1,0:T(8,128)(2,1)}, u32[]{:S(2)}) copy-start(bf16[2048,1024]{1,0:T(8,128)(2,1)} %param.22) | copy-start | bytes 12582916
  97.3 22.2 %copy-start.15 = (f32[128]{0:T(128)S(1)}, f32[128]{0:T(128)}, u32[]{:S(2)}) copy-start(f32[128]{0:T(128)} %param.32) | copy-start | bytes 1540
  106.8 12.7 %all-to-all-start.2 = ((bf16[8,1,128,128]{3,2,1,0:T(8,128)(2,1)}), bf16[8,1,128,128]{3,2,1,0:T(8,128)(2,1)S(1)}, u32[]{:S(2)}, u32[]{:S(2)}) async-start(bf16[8,1,128,128]{3,2,1,0:T(8,128)(2,1)} %shard_map.164), calls=%async_computation.2 | async-start | bytes 524288 | tf_op jit(solution)/shard_map/all_to_all | solution.py:294
  111.1 5.6 %collective-permute-start.5 = (bf16[3,2048]{1,0:T(4,128)(2,1)}, bf16[3,2048]{1,0:T(4,128)(2,1)S(1)}, u32[]{:S(2)}, u32[]{:S(2)}) collective-permute-start(bf16[3,2048]{1,0:T(4,128)(2,1)} %pad_maximum_fusion.2), channel_id=1, source_target_pairs={{0,4},{4,8},{8,12},{12,16},{16,20},{20,24},{24,28},{1,5},{5,9},{9,... | collective-permute-start | bytes 36872 | tf_op jit(solution)/shard_map/ppermute | solution.py:17
  119.6 1.6 copy-start.16
  123.6 3.2 %copy-start.41 = (bf16[1024,2048]{1,0:T(8,128)(2,1)S(1)}, bf16[1024,2048]{1,0:T(8,128)(2,1)}, u32[]{:S(2)}) copy-start(bf16[1024,2048]{1,0:T(8,128)(2,1)} %param.33) | copy-start | bytes 12582916
  126.8 2.3 %copy-start.3 = (bf16[512,1024]{1,0:T(8,128)(2,1)S(1)}, bf16[512,1024]{1,0:T(8,128)(2,1)}, u32[]{:S(2)}) copy-start(bf16[512,1024]{1,0:T(8,128)(2,1)} %copy-done.2) | copy-start | bytes 3145732
  126.8 2.3 %copy-start.7 = (bf16[512,512]{1,0:T(8,128)(2,1)S(1)}, bf16[512,512]{1,0:T(8,128)(2,1)}, u32[]{:S(2)}) copy-start(bf16[512,512]{1,0:T(8,128)(2,1)} %copy-done.6) | copy-start | bytes 1572868
  126.8 2.3 %copy-start.9 = (bf16[512,512]{1,0:T(8,128)(2,1)S(1)}, bf16[512,512]{1,0:T(8,128)(2,1)}, u32[]{:S(2)}) copy-start(bf16[512,512]{1,0:T(8,128)(2,1)} %copy-done.8) | copy-start | bytes 1572868
  129.1 24.1 %collective-permute-start.3 = (bf16[256,2048]{1,0:T(8,128)(2,1)}, bf16[256,2048]{1,0:T(8,128)(2,1)}, u32[]{:S(2)}, u32[]{:S(2)}) collective-permute-start(bf16[256,2048]{1,0:T(8,128)(2,1)} %convolution_convert_fusion.2), channel_id=1, source_target_pairs={{0,1},{1,0},{2,3},{3,2},{4,5},{5,4},{6,7},{7,6},{8,9},{9,8},{10,11... | collective-permute-start | bytes 3145736 | tf_op jit(solution)/shard_map/ppermute | solution.py:321
  149.4 18.9 %all-to-all-start.3 = ((bf16[8,1,128,256]{3,2,1,0:T(8,128)(2,1)}), bf16[8,1,128,256]{3,2,1,0:T(8,128)(2,1)S(1)}, u32[]{:S(2)}, u32[]{:S(2)}) async-start(bf16[8,1,128,256]{3,2,1,0:T(8,128)(2,1)} %bitcast.147), calls=%async_computation.3 | async-start | bytes 1048576 | tf_op jit(solution)/shard_map/all_to_all | solution.py:291
  153.2 5.6 %copy-start.26 = (bf16[512,2048]{1,0:T(8,128)(2,1)S(1)}, bf16[512,2048]{1,0:T(8,128)(2,1)}, u32[]{:S(2)}) copy-start(bf16[512,2048]{1,0:T(8,128)(2,1)} %copy-done.24) | copy-start | bytes 6291460
  153.2 5.6 %copy-start.40 = (bf16[2048,1024]{1,0:T(8,128)(2,1)S(1)}, bf16[2048,1024]{1,0:T(8,128)(2,1)}, u32[]{:S(2)}) copy-start(bf16[2048,1024]{1,0:T(8,128)(2,1)} %param.23) | copy-start | bytes 12582916
  158.3 15.6 %collective-permute-start.4 = (bf16[128,2048]{1,0:T(8,128)(2,1)}, bf16[128,2048]{1,0:T(8,128)(2,1)}, u32[]{:S(2)}, u32[]{:S(2)}) collective-permute-start(bf16[128,2048]{1,0:T(8,128)(2,1)} %fusion.9), channel_id=1, source_target_pairs={{0,2},{1,3},{2,0},{3,1},{4,6},{5,7},{6,4},{7,5},{8,10},{9,11},{10,... | collective-permute-start | bytes 1572872 | tf_op jit(solution)/shard_map/ppermute | solution.py:334
  170.1 12.9 %copy-start.22 = (bf16[512,1024]{1,0:T(8,128)(2,1)S(1)}, bf16[512,1024]{1,0:T(8,128)(2,1)}, u32[]{:S(2)}) copy-start(bf16[512,1024]{1,0:T(8,128)(2,1)} %copy-done.21) | copy-start | bytes 3145732
  170.1 12.9 %all-to-all-start.4 = ((bf16[8,1,128,128]{3,2,1,0:T(8,128)(2,1)}), bf16[8,1,128,128]{3,2,1,0:T(8,128)(2,1)S(1)}, u32[]{:S(2)}, u32[]{:S(2)}) async-start(bf16[8,1,128,128]{3,2,1,0:T(8,128)(2,1)} %shard_map.167), calls=%async_computation.4 | async-start | bytes 524288 | tf_op jit(solution)/shard_map/all_to_all | solution.py:294
  185.8 2.4 %copy-start.42 = (bf16[1024,2048]{1,0:T(8,128)(2,1)S(1)}, bf16[1024,2048]{1,0:T(8,128)(2,1)}, u32[]{:S(2)}) copy-start(bf16[1024,2048]{1,0:T(8,128)(2,1)} %param.33) | copy-start | bytes 12582916
  189.5 2.7 %collective-permute-start.6 = (bf16[256,2048]{1,0:T(8,128)(2,1)S(1)}, bf16[256,2048]{1,0:T(8,128)(2,1)S(1)}, u32[]{:S(2)}, u32[]{:S(2)}) collective-permute-start(bf16[256,2048]{1,0:T(8,128)(2,1)S(1)} %convolution_convert_fusion), channel_id=1, source_target_pairs={{0,1},{1,0},{2,3},{3,2},{4,5},{5,4},{6,7},{7,6},{8,9},{9,8},{10,11... | collective-permute-start | bytes 3145736 | tf_op jit(solution)/shard_map/ppermute | solution.py:321
  193.5 14.2 %copy-start.30 = (bf16[128,2048]{1,0:T(8,128)(2,1)S(1)}, bf16[128,2048]{1,0:T(8,128)(2,1)}, u32[]{:S(2)}) copy-start(bf16[128,2048]{1,0:T(8,128)(2,1)} %fusion.8) | copy-start | bytes 1572868
  193.6 14.0 %collective-permute-start.7 = (bf16[128,2048]{1,0:T(8,128)(2,1)S(1)}, bf16[128,2048]{1,0:T(8,128)(2,1)S(1)}, u32[]{:S(2)}, u32[]{:S(2)}) collective-permute-start(bf16[128,2048]{1,0:T(8,128)(2,1)S(1)} %fusion.10), channel_id=1, source_target_pairs={{0,2},{1,3},{2,0},{3,1},{4,6},{5,7},{6,4},{7,5},{8,10},{9,11},{10,... | collective-permute-start | bytes 1572872 | tf_op jit(solution)/shard_map/ppermute | solution.py:334
  (13 other events, 14.6 us)
Sparse Core Ops, SparseCore 0:
  9.1 25.6 all-gather.4
  36.4 22.5 all-gather.6
